TPU v7x, 512 devices: a whole 4x8x8 slice. The times are simulated.
512 devices in a mesh: dp: 4 (over x), group: 16 (over y, z_lo), head: 8 (over z_hi, core).
Axes of the slice: x: 4, y: 8, z: 8 (z_hi: 4, z_lo: 2; z = z_hi * 2 + z_lo), core: 2. Of those that a mesh axis runs over, the one named last changes fastest.
Arguments:
- queries: bfloat16 [4, 16, 1024, 2048], P('dp', 'group', 'head'), may hold values from -130 to 130
- keys: bfloat16 [4, 16, 1024, 2048], P('dp', 'group', 'head'), may hold values from -4 to 4
- values: bfloat16 [4, 16, 1024, 2048], P('dp', 'group', 'head'), may hold values from -6 to 6
- noise: bfloat16 [4, 16, 1024, 3072], P('dp', 'group', 'head'), may hold values from -6 to 6
- projection: bfloat16 [2048, 3072], P('head', 'dp'), may hold values from -0.125 to 0.125
- rewards: float32 [4, 16], P('dp', 'group'), may hold values from -40 to 40
- counts: int32 [4], P('dp'), may hold values from 64 to 128, as said below
- step_index: int32 [1], replicated, may hold values from 1 to 49
Outputs:
- grad_queries: bfloat16 [4, 16, 1024, 2048], P('dp', 'group', 'head')
- grad_keys: bfloat16 [4, 16, 1024, 2048], P('dp', 'group', 'head')
- grad_values: bfloat16 [4, 16, 1024, 2048], P('dp', 'group', 'head')
- grad_projection: float32 [2048, 3072], P('head', 'dp')
Inputs may be any that keep to these rules, and one draw needn't show every extreme that they name: `counts`: one prompt has 128 live text tokens and another 128 // 2.
All inputs are finite; a program needn't handle non-finite values.
Results may differ from a plain program's by a relative error of at most 0.014.
The roundings to bfloat16 on the way count: a program that leaves them out, or rounds other values in their place, can miss the bound.
Values may be sent and summed in bfloat16 or wider, within the bound.
A program may use at most 64 MiB of HBM per device.

v0:
```python
import jax
import jax.numpy as jnp
from jax import lax
from jax.sharding import PartitionSpec as P

HD = 128
TXT = 128
NSTEPS = 50


shift_factor = 7.0
noise_level = 0.7
loss_scale = 64.0
spread_floor = 0.25
masked_score = -1e30


def step_factor(step_index, rollout_count):
    current = step_index[0].astype(jnp.float32)

    def level_at(position):
        remain = 1.0 - position / NSTEPS
        return shift_factor * remain / (1.0 + (shift_factor - 1.0) * remain)

    stride = level_at(current) - level_at(current + 1.0)
    return loss_scale * jnp.sqrt(stride) / (noise_level * rollout_count)


def text_mask(live_text, length):
    position = jnp.arange(length, dtype=jnp.int32)
    return position < length - TXT + live_text


def head_grads(query_head, key_head, value_head, dout_head, usable):
    factor = HD ** (-0.5)
    scores = jnp.dot(query_head, key_head.T, preferred_element_type=jnp.float32) * factor
    scores = jnp.where(usable[None, :], scores, masked_score)
    row_peak = jnp.max(scores, axis=1, keepdims=True)
    logsum = row_peak + jnp.log(jnp.sum(jnp.exp(scores - row_peak), axis=1, keepdims=True))
    attn_probs = jnp.exp(scores - logsum)
    probs_low = attn_probs.astype(jnp.bfloat16)
    output = jnp.dot(probs_low, value_head, preferred_element_type=jnp.float32).astype(jnp.bfloat16)
    row_dot = jnp.sum(
        dout_head.astype(jnp.float32) * output.astype(jnp.float32), axis=1, keepdims=True
    )
    dprobs = jnp.dot(dout_head, value_head.T, preferred_element_type=jnp.float32)
    dscores = (attn_probs * (dprobs - row_dot)).astype(jnp.bfloat16)
    grad_query = jnp.dot(dscores, key_head, preferred_element_type=jnp.float32) * factor
    grad_key = jnp.dot(dscores.T, query_head, preferred_element_type=jnp.float32) * factor
    grad_value = jnp.dot(probs_low.T, dout_head, preferred_element_type=jnp.float32)
    return (output, grad_query, grad_key, grad_value)


def split_heads(matrix):
    return matrix.reshape(matrix.shape[0], -1, HD).transpose(1, 0, 2)


def join_heads(stack):
    return stack.transpose(1, 0, 2).reshape(stack.shape[1], -1)


def local(queries, keys, values, noise, projection, rewards, counts, step_index):
    group_count = lax.axis_size("group")
    base = step_factor(step_index, group_count)
    reward_avg = lax.psum(rewards, "group") / group_count
    variance = lax.psum((rewards - reward_avg) ** 2, "group") / group_count
    advantage = (rewards - reward_avg) / jnp.maximum(jnp.sqrt(variance), spread_floor)
    factor = (base * advantage)[0, 0]
    head_query, head_key, head_value = (
        lax.all_to_all(queries, "head", split_axis=3, concat_axis=2, tiled=True),
        lax.all_to_all(keys, "head", split_axis=3, concat_axis=2, tiled=True),
        lax.all_to_all(values, "head", split_axis=3, concat_axis=2, tiled=True),
    )
    head_query = head_query[0, 0]
    head_key = head_key[0, 0]
    head_value = head_value[0, 0]
    length = head_query.shape[0]
    whole_noise = lax.all_gather(noise, "head", axis=2, tiled=True)[0, 0]
    columns = whole_noise
    dout = lax.dot_general(
        columns,
        lax.all_gather(projection, "dp", axis=1, tiled=True),
        (((1,), (1,)), ((), ())),
        preferred_element_type=jnp.float32,
    ).astype(jnp.bfloat16)
    usable = text_mask(counts[0], length)

    def one_head(operands):
        return head_grads(operands[0], operands[1], operands[2], operands[3], usable)

    outputs, grad_query, grad_key, grad_value = lax.map(
        one_head,
        (
            split_heads(head_query),
            split_heads(head_key),
            split_heads(head_value),
            split_heads(dout),
        ),
    )
    outputs = join_heads(outputs)
    low_query = (factor * join_heads(grad_query)).astype(jnp.bfloat16)[None, None]
    low_key = (factor * join_heads(grad_key)).astype(jnp.bfloat16)[None, None]
    low_value = (factor * join_heads(grad_value)).astype(jnp.bfloat16)[None, None]
    grad_queries, grad_keys, grad_values = (
        lax.all_to_all(low_query, "head", split_axis=2, concat_axis=3, tiled=True),
        lax.all_to_all(low_key, "head", split_axis=2, concat_axis=3, tiled=True),
        lax.all_to_all(low_value, "head", split_axis=2, concat_axis=3, tiled=True),
    )
    columns = whole_noise
    shares = lax.psum_scatter(
        factor
        * lax.dot_general(
            columns, outputs, (((0,), (0,)), ((), ())), preferred_element_type=jnp.float32
        ),
        "dp",
        scatter_dimension=0,
        tiled=True,
    )
    shares = lax.psum(shares, "group")
    return (grad_queries, grad_keys, grad_values, shares.T)


def solution(mesh):
    in_specs = (
        P("dp", "group", "head", None),
        P("dp", "group", "head", None),
        P("dp", "group", "head", None),
        P("dp", "group", "head", None),
        P("head", "dp"),
        P("dp", "group"),
        P("dp"),
        P(),
    )
    out_specs = (
        P("dp", "group", "head", None),
        P("dp", "group", "head", None),
        P("dp", "group", "head", None),
        P("head", "dp"),
    )
    return jax.shard_map(local, mesh=mesh, in_specs=in_specs, out_specs=out_specs, check_vma=False)
```

profile of v0, /device:TPU:2, one launch (start us, length us, event | category | flops | bytes accessed | tf_op | source)
XLA Modules:
  0.0 446.9 jit_solution(7999133112199480326)
XLA Ops:
  11.6 11.5 %reduce = bf16[2048,128]{1,0:T(8,128)(2,1)S(1)} reduce(bf16[2048,1,1,128]{3,2,1,0:T(2,128)(2,1)S(1)} %bitcast.166, bf16[]{:T(256)} %broadcast.58), dimensions={1,2}, to_apply=%bitcast.106.reduce_sub_computation | reduce | bytes 1048578
  24.0 10.3 %all-to-all-start = ((bf16[8,2,16384]{2,1,0:T(2,128)(2,1)}), bf16[8,2,16384]{2,1,0:T(2,128)(2,1)S(1)}, u32[]{:S(2)}, u32[]{:S(2)}) async-start(bf16[8,2,16384]{2,1,0:T(2,128)(2,1)} %reshape.113), calls=%async_computation | async-start | bytes 1048576 | tf_op jit(solution)/shard_map/all_to_all | solution.py:70
  35.1 11.5 %reduce.1 = bf16[2048,128]{1,0:T(8,128)(2,1)S(1)} reduce(bf16[2048,1,1,128]{3,2,1,0:T(2,128)(2,1)S(1)} %bitcast.170, bf16[]{:T(256)} %broadcast.58), dimensions={1,2}, to_apply=%bitcast.108.reduce_sub_computation | reduce | bytes 1048578
  47.5 5.2 %all-to-all-done = bf16[8,2,16384]{2,1,0:T(2,128)(2,1)S(1)} async-done(((bf16[8,2,16384]{2,1,0:T(2,128)(2,1)}), bf16[8,2,16384]{2,1,0:T(2,128)(2,1)S(1)}, u32[]{:S(2)}, u32[]{:S(2)}) %all-to-all-start) | async-done | bytes 524320 | tf_op jit(solution)/shard_map/all_to_all | solution.py:70
  52.7 15.1 %all-to-all-start.1 = ((bf16[8,2,16384]{2,1,0:T(2,128)(2,1)}), bf16[8,2,16384]{2,1,0:T(2,128)(2,1)S(1)}, u32[]{:S(2)}, u32[]{:S(2)}) async-start(bf16[8,2,16384]{2,1,0:T(2,128)(2,1)} %reshape.115), calls=%async_computation.1 | async-start | bytes 1048576 | tf_op jit(solution)/shard_map/all_to_all | solution.py:71
  68.6 11.5 %reduce.2 = bf16[2048,128]{1,0:T(8,128)(2,1)S(1)} reduce(bf16[2048,1,1,128]{3,2,1,0:T(2,128)(2,1)S(1)} %bitcast.171, bf16[]{:T(256)} %broadcast.58), dimensions={1,2}, to_apply=%bitcast.110.reduce_sub_computation | reduce | bytes 1048578
  81.0 14.7 %all-to-all-done.1 = bf16[8,2,16384]{2,1,0:T(2,128)(2,1)S(1)} async-done(((bf16[8,2,16384]{2,1,0:T(2,128)(2,1)}), bf16[8,2,16384]{2,1,0:T(2,128)(2,1)S(1)}, u32[]{:S(2)}, u32[]{:S(2)}) %all-to-all-start.1) | async-done | bytes 524320 | tf_op jit(solution)/shard_map/all_to_all | solution.py:71
  95.7 3.5 all-to-all-start.2
  99.3 58.6 %psum.21 = f32[1,1]{1,0:T(1,128)} all-reduce(f32[1,1]{1,0:T(1,128)} %param.15), channel_id=1, replica_groups=mesh['dp'=4,'group'=16,'head'=8] {'group'}, use_global_device_ids=true, to_apply=%region_0.0 | all-reduce | flops 1 | bytes 8 | tf_op jit(solution)/shard_map/psum | solution.py:65
  159.2 33.3 %psum.22 = f32[1,1]{1,0:T(1,128)} all-reduce(f32[1,1]{1,0:T(1,128)S(6)} %integer_pow.3), channel_id=1, replica_groups=mesh['dp'=4,'group'=16,'head'=8] {'group'}, use_global_device_ids=true, to_apply=%region_1.0 | all-reduce | flops 1 | bytes 8 | tf_op jit(solution)/shard_map/psum | solution.py:66
  199.1 5.0 %fusion.42 = bf16[1024,256]{0,1:T(8,128)(2,1)S(1)} fusion(bf16[256,3072]{1,0:T(8,128)(2,1)} %all-gather.5.cloned.1.call-done, bf16[1,1,1024,3072]{3,2,1,0:T(8,128)(2,1)} %all-gather.3.cloned.1.call-done), kind=kOutput, calls=%fused_computation.49 | convolution fusion | flops 1610874880 | bytes 8388608 | tf_op jit(solution)/shard_map/dot_general | solution.py:80
  204.2 24.3 %while.17 = (s32[]{:T(128)}, bf16[2,1024,128]{1,2,0:T(8,128)(2,1)}, f32[2,1024,128]{1,2,0:T(8,128)}, f32[2,1024,128]{1,2,0:T(8,128)}, f32[2,1024,128]{1,2,0:T(8,...) while((s32[]{:T(128)}, bf16[2,1024,128]{1,2,0:T(8,128)(2,1)}, ...), condition=%wide.region_6.7_spmd.clone, body=%wide.region_2.6_spmd.clone.sunk | while | flops 1633549312 | bytes 36231304 | solution.py:91
  218.1 2.9 bitcast_dynamic-update-slice_fusion.2
  228.5 6.5 %fusion.39 = f32[3072,256]{0,1:T(8,128)} fusion(bf16[1024,256]{0,1:T(8,128)(2,1)} %bitcast.25, bf16[1,1,1024,3072]{3,2,1,0:T(8,128)(2,1)} %all-gather.3.cloned.1.call-done, f32[]{:T(128)} %bitcast.1), kind=kOutput, calls=%fused_computation.48 | convolution fusion | flops 1611399168 | bytes 9961476 | tf_op jit(solution)/shard_map/dot_general | solution.py:112
  236.0 3.8 reduce.3
  240.7 7.1 %all-to-all-start.3 = ((bf16[8,2,16384]{2,1,0:T(2,128)(2,1)}), bf16[8,2,16384]{2,1,0:T(2,128)(2,1)S(1)}, u32[]{:S(2)}, u32[]{:S(2)}) async-start(bf16[8,2,16384]{2,1,0:T(2,128)(2,1)} %reshape.119), calls=%async_computation.3 | async-start | bytes 1048576 | tf_op jit(solution)/shard_map/all_to_all | solution.py:105
  250.1 3.8 reduce.4
  254.8 11.2 %all-to-all-done.3 = bf16[8,2,16384]{2,1,0:T(2,128)(2,1)S(1)} async-done(((bf16[8,2,16384]{2,1,0:T(2,128)(2,1)}), bf16[8,2,16384]{2,1,0:T(2,128)(2,1)S(1)}, u32[]{:S(2)}, u32[]{:S(2)}) %all-to-all-start.3) | async-done | bytes 524320 | tf_op jit(solution)/shard_map/all_to_all | solution.py:105
  266.0 3.7 all-to-all-start.4
  270.6 3.8 reduce.5
  275.3 12.2 %all-to-all-done.4 = bf16[8,2,16384]{2,1,0:T(2,128)(2,1)S(1)} async-done(((bf16[8,2,16384]{2,1,0:T(2,128)(2,1)}), bf16[8,2,16384]{2,1,0:T(2,128)(2,1)S(1)}, u32[]{:S(2)}, u32[]{:S(2)}) %all-to-all-start.4) | async-done | bytes 524320 | tf_op jit(solution)/shard_map/all_to_all | solution.py:106
  287.5 3.5 all-to-all-start.5
  295.5 12.4 %all-to-all-done.5 = bf16[8,2,16384]{2,1,0:T(2,128)(2,1)S(1)} async-done(((bf16[8,2,16384]{2,1,0:T(2,128)(2,1)}), bf16[8,2,16384]{2,1,0:T(2,128)(2,1)S(1)}, u32[]{:S(2)}, u32[]{:S(2)}) %all-to-all-start.5) | async-done | bytes 524320 | tf_op jit(solution)/shard_map/all_to_all | solution.py:107
  309.7 128.2 %all-reduce.2.cloned.1.call-done = f32[256,768]{1,0:T(8,128)} async-done(((f32[256,768]{1,0:T(8,128)}), f32[256,768]{1,0:T(8,128)}) %all-reduce.2.cloned.1.call-update) | async-done | bytes 786448 | tf_op jit(solution)/shard_map/psum | solution.py:119
  (89 shorter events, 49.5 us)
Async XLA Ops:
  7.2 27.2 %copy-start.2 = (bf16[1,1,128,2048]{3,2,1,0:T(8,128)(2,1)S(1)}, bf16[1,1,128,2048]{3,2,1,0:T(8,128)(2,1)}, u32[]{:S(2)}) copy-start(bf16[1,1,128,2048]{3,2,1,0:T(8,128)(2,1)} %param.11) | copy-start | bytes 1572868
  7.2 192.0 %all-gather.5.cloned.1.call-start = ((), (), s32[]{:S(2)}) async-start(), calls=%async_computation.8 | async-start | bytes 1966080 | tf_op jit(solution)/shard_map/all_gather | solution.py:82
  7.9 191.2 %all-gather.3.cloned.1.call-start = ((), (), s32[]{:S(2)}) async-start(), calls=%async_computation.7 | async-start | bytes 7077888 | tf_op jit(solution)/shard_map/all_gather | solution.py:78
  11.6 56.3 %copy-start.3 = (bf16[1,1,128,2048]{3,2,1,0:T(8,128)(2,1)S(1)}, bf16[1,1,128,2048]{3,2,1,0:T(8,128)(2,1)}, u32[]{:S(2)}) copy-start(bf16[1,1,128,2048]{3,2,1,0:T(8,128)(2,1)} %param.12) | copy-start | bytes 1572868
  24.0 28.7 %all-to-all-start = ((bf16[8,2,16384]{2,1,0:T(2,128)(2,1)}), bf16[8,2,16384]{2,1,0:T(2,128)(2,1)S(1)}, u32[]{:S(2)}, u32[]{:S(2)}) async-start(bf16[8,2,16384]{2,1,0:T(2,128)(2,1)} %reshape.113), calls=%async_computation | async-start | bytes 1048576 | tf_op jit(solution)/shard_map/all_to_all | solution.py:70
  52.7 43.0 %all-to-all-start.1 = ((bf16[8,2,16384]{2,1,0:T(2,128)(2,1)}), bf16[8,2,16384]{2,1,0:T(2,128)(2,1)S(1)}, u32[]{:S(2)}, u32[]{:S(2)}) async-start(bf16[8,2,16384]{2,1,0:T(2,128)(2,1)} %reshape.115), calls=%async_computation.1 | async-start | bytes 1048576 | tf_op jit(solution)/shard_map/all_to_all | solution.py:71
  95.7 101.4 %all-to-all-start.2 = ((bf16[8,2,16384]{2,1,0:T(2,128)(2,1)}), bf16[8,2,16384]{2,1,0:T(2,128)(2,1)S(1)}, u32[]{:S(2)}, u32[]{:S(2)}) async-start(bf16[8,2,16384]{2,1,0:T(2,128)(2,1)} %reshape.117), calls=%async_computation.2 | async-start | bytes 1048576 | tf_op jit(solution)/shard_map/all_to_all | solution.py:72
  99.2 191.9 %reduce-scatter.2.cloned.1.call-start = ((), (), s32[]{:S(2)}) async-start(), calls=%async_computation.9 | async-start | bytes 3932160 | tf_op jit(solution)/shard_map/reduce_scatter | solution.py:110
  228.5 6.6 %copy-start.1 = (f32[2,1024,128]{1,2,0:T(8,128)S(1)}, f32[2,1024,128]{1,2,0:T(8,128)}, u32[]{:S(2)}) copy-start(f32[2,1024,128]{1,2,0:T(8,128)} %get-tuple-element.59) | copy-start | bytes 3145732
  235.0 12.7 %copy-start = (f32[2,1024,128]{1,2,0:T(8,128)S(1)}, f32[2,1024,128]{1,2,0:T(8,128)}, u32[]{:S(2)}) copy-start(f32[2,1024,128]{1,2,0:T(8,128)} %get-tuple-element.60) | copy-start | bytes 3145732
  240.7 25.3 %all-to-all-start.3 = ((bf16[8,2,16384]{2,1,0:T(2,128)(2,1)}), bf16[8,2,16384]{2,1,0:T(2,128)(2,1)S(1)}, u32[]{:S(2)}, u32[]{:S(2)}) async-start(bf16[8,2,16384]{2,1,0:T(2,128)(2,1)} %reshape.119), calls=%async_computation.3 | async-start | bytes 1048576 | tf_op jit(solution)/shard_map/all_to_all | solution.py:105
  266.0 21.6 %all-to-all-start.4 = ((bf16[8,2,16384]{2,1,0:T(2,128)(2,1)}), bf16[8,2,16384]{2,1,0:T(2,128)(2,1)S(1)}, u32[]{:S(2)}, u32[]{:S(2)}) async-start(bf16[8,2,16384]{2,1,0:T(2,128)(2,1)} %reshape.121), calls=%async_computation.4 | async-start | bytes 1048576 | tf_op jit(solution)/shard_map/all_to_all | solution.py:106
  287.5 20.3 %all-to-all-start.5 = ((bf16[8,2,16384]{2,1,0:T(2,128)(2,1)}), bf16[8,2,16384]{2,1,0:T(2,128)(2,1)S(1)}, u32[]{:S(2)}, u32[]{:S(2)}) async-start(bf16[8,2,16384]{2,1,0:T(2,128)(2,1)} %reshape.123), calls=%async_computation.5 | async-start | bytes 1048576 | tf_op jit(solution)/shard_map/all_to_all | solution.py:107
  291.1 146.9 %all-reduce.2.cloned.1.call-start = ((), (), s32[]{:S(2)}) async-start(), calls=%async_computation.10 | async-start | bytes 1572864 | tf_op jit(solution)/shard_map/psum | solution.py:119
Sparse Core Ops, SparseCore 0:
  10.1 35.4 all-gather.4
  47.7 97.6 all-gather.2
  235.1 43.4 reduce-scatter.1
  294.5 143.3 all-reduce.1
where the time goes:
time: 455 us; the launch traced here: 447 us
  waiting for transfers between devices  186 us (41%)
  blocking collectives  91.9 us (20%)
  other arithmetic  49.5 us (11%)
  starting transfers between devices  43.4 us (10%)
  matrix products  30.8 us (7%)
  local copies, waits for them, and re-layouts  27.4 us (6%)
  between operations  18.1 us (4%)
    psum x1, waiting for transfers between devices, local(): shares = lax.psum(shares, 'group')  128 us
    psum x1, blocking collectives, local(): reward_avg = lax.psum(rewards, 'group') / group_count  58.6 us
    unnamed x6, other arithmetic  45.9 us
    psum x1, blocking collectives, local(): variance = lax.psum((rewards - reward_avg) ** 2, 'group') / group_count  33.3 us
    unnamed x34, local copies, waits for them, and re-layouts  18.7 us
    all_to_all x1, starting transfers between devices, local(): lax.all_to_all(keys, 'head', split_axis=3, concat_axis=2, tiled=True)  15.1 us
    all_to_all x1, waiting for transfers between devices, local(): lax.all_to_all(keys, 'head', split_axis=3, concat_axis=2, tiled=True)  14.7 us
    all_to_all x1, waiting for transfers between devices, local(): lax.all_to_all(low_value, 'head', split_axis=2, concat_axis=3, tiled=True)  12.4 us
  transfers between devices with their start and end apart: 10, of which 6 were waited for; matrix products, arithmetic and copies ran while one was open for 16% of the time, Pallas kernels for 0%

commit v1 on v0

v1 whole, which is shorter than its diff:
```python
import functools
import math

import jax
import jax.numpy as jnp
from jax import lax
from jax.experimental import pallas as pl
from jax.experimental.pallas import tpu as pltpu
from jax.sharding import PartitionSpec as P

HD = 128
TXT = 128
NSTEPS = 50
SEQ = 1024
HW = 2048
D = 3072
HEADS = 8
DP = 4
GROUP = 16
TOK = SEQ // HEADS
FEAT = HW // HEADS
COLS = D // DP
CH = 256
NCH = SEQ // CH

shift_factor = 7.0
noise_level = 0.7
loss_scale = 64.0
spread_floor = 0.25
masked_score = -1e30

BF = jnp.bfloat16
F32 = jnp.float32
MESH = pl.DeviceIdType.MESH


def step_factor(step_index, rollout_count):
    current = step_index[0].astype(F32)

    def level_at(position):
        remain = 1.0 - position / NSTEPS
        return shift_factor * remain / (1.0 + (shift_factor - 1.0) * remain)

    stride = level_at(current) - level_at(current + 1.0)
    return loss_scale * jnp.sqrt(stride) / (noise_level * rollout_count)


def dot(a, b, ca, cb):
    return lax.dot_general(a, b, (((ca,), (cb,)), ((), ())), preferred_element_type=F32)


def kernel(
    q_in, k_in, v_in, n_in, p_in, rew_in, base_in, bias_in,
    gq_out, gk_out, gv_out, gp_out,
    qkv, nbuf, pbuf, rbuf, probs, kt, vt, out_t, dout_t, wacc, wlow, xrecv, grecv, glow, agbuf,
    grads, acc_k, acc_v,
    s_qkv, r_qkv, s_n, r_n, s_nf, r_nf, s_ns, r_ns, s_p, r_p, s_rew, r_rew,
    s_x, r_x, s_g, r_g, s_a, r_a, s_o, r_o,
):
    x = lax.axis_index("dp")
    g = lax.axis_index("group")
    me = lax.axis_index("head")
    core = lax.rem(me, 2)
    sib = me + 1 - 2 * core
    zup = lax.rem(me + 2, HEADS)
    zdn = lax.rem(me + HEADS - 2, HEADS)
    zop = lax.rem(me + 4, HEADS)

    def remote(src, dst, ssem, rsem, dev):
        return pltpu.make_async_remote_copy(
            src_ref=src, dst_ref=dst, send_sem=ssem, recv_sem=rsem, device_id=dev, device_id_type=MESH
        )

    def head_peer(r):
        return (x, g, lax.rem(me + r, HEADS))

    def dp_peer(r):
        return (lax.rem(x + r, DP), g, me)

    def group_peer(r):
        return (x, lax.rem(g + r, GROUP), me)

    def rows(block, size):
        return pl.ds(pl.multiple_of(block * size, size), size)

    barrier = pltpu.get_barrier_semaphore()

    def greet(count, peer):
        def body(r, carry):
            pl.semaphore_signal(barrier, inc=1, device_id=peer(r), device_id_type=MESH)
            return carry

        lax.fori_loop(1, count, body, 0)

    greet(HEADS, head_peer)
    greet(DP, dp_peer)
    greet(GROUP, group_peer)
    pl.semaphore_wait(barrier, HEADS + DP + GROUP - 3)

    mine = n_in.at[0, 0]
    own = nbuf.at[rows(me, TOK)]
    c_up = remote(mine, own, s_n.at[0], r_n.at[0], (x, g, zup))
    c_dn = remote(mine, own, s_n.at[1], r_n.at[1], (x, g, zdn))
    c_sib = remote(mine, own, s_ns.at[0], r_ns.at[0], (x, g, sib))
    c_own = pltpu.make_async_copy(mine, own, s_n.at[2])
    c_up.start()
    c_dn.start()
    c_sib.start()
    c_own.start()

    pcols = pl.ds(pl.multiple_of(x * COLS, COLS), COLS)

    def p_copy(r):
        return remote(p_in, pbuf.at[:, pcols], s_p.at[r], r_p.at[r], dp_peer(r))

    def rew_copy(r):
        return remote(rew_in, rbuf.at[r], s_rew.at[r], r_rew.at[r], group_peer(r))

    def start_all(count, make):
        def body(r, carry):
            make(r).start()
            return carry

        lax.fori_loop(1, count, body, 0)

    def wait_recv(count, make):
        def body(r, carry):
            make(r).wait_recv()
            return carry

        lax.fori_loop(1, count, body, 0)

    def wait_send(count, make):
        def body(r, carry):
            make(r).wait_send()
            return carry

        lax.fori_loop(1, count, body, 0)

    start_all(DP, p_copy)
    p_own = pltpu.make_async_copy(p_in, pbuf.at[:, pcols], s_p.at[0])
    p_own.start()

    ins = (q_in, k_in, v_in)

    def qkv_copy(a, h):
        def make(r):
            dst = lax.rem(me + r, HEADS)
            cols = pl.ds(pl.multiple_of(dst * FEAT + h * HD, HD), HD)
            return remote(
                ins[a].at[0, 0, :, cols], qkv.at[a, h, rows(me, TOK)],
                s_qkv.at[a, h, r], r_qkv.at[a, h, r], (x, g, dst),
            )

        return make

    def qkv_own(a, h):
        cols = pl.ds(pl.multiple_of(me * FEAT + h * HD, HD), HD)
        return pltpu.make_async_copy(
            ins[a].at[0, 0, :, cols], qkv.at[a, h, rows(me, TOK)], s_qkv.at[a, h, 0]
        )

    for h in range(2):
        for a in range(3):
            start_all(HEADS, qkv_copy(a, h))
            qkv_own(a, h).start()
    start_all(GROUP, rew_copy)

    wait_recv(GROUP, rew_copy)
    rbuf[0] = rew_in[...]
    rewards = rbuf[...]
    average = jnp.sum(rewards, axis=0) / GROUP
    variance = jnp.sum((rewards - average[None]) ** 2, axis=0) / GROUP
    factor = base_in[...] * ((rew_in[...] - average) / jnp.maximum(jnp.sqrt(variance), spread_floor))
    factor = factor[0:1, :]

    def forward(sem, source, half, target):
        part = nbuf.at[pl.ds(pl.multiple_of(source * TOK + half * (TOK // 2), TOK // 2), TOK // 2)]
        return remote(part, part, s_nf.at[sem], r_nf.at[sem], (x, g, target))

    def to_sib(slot, source):
        part = nbuf.at[rows(source, TOK)]
        return remote(part, part, s_ns.at[slot], r_ns.at[slot], (x, g, sib))

    f_up = forward(0, zdn, 0, zup)
    f_dn = forward(1, zup, 1, zdn)
    sib_dn = to_sib(1, zdn)
    sib_up = to_sib(2, zup)
    sib_op = to_sib(3, zop)
    c_up.wait_recv()
    f_up.start()
    sib_dn.start()
    c_dn.wait_recv()
    f_dn.start()
    sib_up.start()

    p_own.wait()
    wait_recv(DP, p_copy)

    def make_dout(block):
        tokens = rows(block // 2, CH)
        part = dot(pbuf[...], nbuf[tokens, :], 1, 1)
        dout_t[block // 2] = part.astype(BF)

    def add_weight(block, first):
        pair = block // 2
        lhs = out_t[pair]

        def body(j, carry):
            cols = pl.ds(pl.multiple_of(j * COLS, COLS), COLS)
            part = dot(lhs, nbuf[rows(pair, CH), cols], 1, 0)
            if first:
                wacc[j] = part
            else:
                wacc[j] += part
            return carry

        lax.fori_loop(0, DP, body, 0)

    c_own.wait()
    c_sib.wait_recv()
    make_dout(me)
    sib_dn.wait_recv()
    make_dout(zdn)
    sib_up.wait_recv()
    make_dout(zup)

    scale = HD ** (-0.5)

    def forward_head(h):
        for a in range(3):
            qkv_own(a, h).wait()
            wait_recv(HEADS, qkv_copy(a, h))
        kt[h] = qkv[1, h].T
        vt[h] = qkv[2, h].T

        def body(c, carry):
            qc = qkv[0, h, rows(c, CH), :]
            t = dot(qkv[1, h], qc, 1, 1) * (scale * math.log2(math.e))
            t = jnp.concatenate([t[: SEQ - TXT], t[SEQ - TXT :] + bias_in[...]], axis=0)
            peak = jnp.max(t, axis=0, keepdims=True)
            e = jnp.exp2(t - peak)
            total = jnp.sum(e, axis=0, keepdims=True)
            pr = e * (1.0 / total)
            probs[h, c] = pr
            part = dot(vt[h], pr.astype(BF), 1, 0)
            out_t[c, pl.ds(h * HD, HD), :] = part.astype(BF)
            return carry

        lax.fori_loop(0, NCH, body, 0)

    forward_head(0)
    forward_head(1)
    add_weight(me, True)
    add_weight(zdn, False)
    add_weight(zup, False)

    f_up.wait_recv()
    f_dn.wait_recv()
    sib_op.start()
    sib_op.wait_recv()
    make_dout(zop)
    add_weight(zop, False)
    for j in range(DP):
        wlow[j] = (wacc[j] * factor[0:1, 0:1]).astype(BF)

    def x_copy(r):
        return remote(wlow.at[lax.rem(x + r, DP)], xrecv.at[r], s_x.at[r], r_x.at[r], dp_peer(r))

    start_all(DP, x_copy)

    outs = (gq_out, gk_out, gv_out)

    def out_copy(a, h):
        cols = pl.ds(pl.multiple_of(me * FEAT + h * HD, HD), HD)

        def make(r):
            dst = lax.rem(me + r, HEADS)
            return remote(
                grads.at[a, h, rows(dst, TOK)], outs[a].at[0, 0, :, cols],
                s_o.at[a, h, r], r_o.at[a, h, r], (x, g, dst),
            )

        return make

    def out_own(a, h):
        cols = pl.ds(pl.multiple_of(me * FEAT + h * HD, HD), HD)
        return pltpu.make_async_copy(
            grads.at[a, h, rows(me, TOK)], outs[a].at[0, 0, :, cols], s_o.at[a, h, 0]
        )

    def backward_head(h):
        acc_k[...] = jnp.zeros_like(acc_k)
        acc_v[...] = jnp.zeros_like(acc_v)

        def body(c, carry):
            pr = probs[h, c]
            dt = dout_t[c, pl.ds(h * HD, HD), :]
            ot = out_t[c, pl.ds(h * HD, HD), :]
            row_dot = jnp.sum(dt.astype(F32) * ot.astype(F32), axis=0, keepdims=True)
            dp = dot(qkv[2, h], dt, 1, 0)
            ds = (pr * (dp - row_dot)).astype(BF)
            gqt = dot(kt[h], ds, 1, 0)
            grads[0, h, rows(c, CH), :] = (gqt.T * (scale * factor)).astype(BF)
            acc_k[...] += dot(ds, qkv[0, h, rows(c, CH), :], 1, 0)
            acc_v[...] += dot(pr.astype(BF), dt, 1, 1)
            return carry

        lax.fori_loop(0, NCH, body, 0)
        grads[1, h] = (acc_k[...] * (scale * factor)).astype(BF)
        grads[2, h] = (acc_v[...] * factor).astype(BF)
        for a in range(3):
            start_all(HEADS, out_copy(a, h))
            out_own(a, h).start()

    backward_head(0)
    backward_head(1)

    wait_recv(DP, x_copy)
    total = wlow[x].astype(F32)
    for r in range(1, DP):
        total = total + xrecv[r].astype(F32)
    glow[...] = total.reshape(GROUP, 16, COLS).astype(BF)

    def g_copy(r):
        return remote(glow.at[lax.rem(g + r, GROUP)], grecv.at[r], s_g.at[r], r_g.at[r], group_peer(r))

    start_all(GROUP, g_copy)
    wait_recv(GROUP, g_copy)
    part = glow[g].astype(F32)
    for r in range(1, GROUP):
        part = part + grecv[r].astype(F32)
    agbuf[g] = part.astype(BF)

    def a_copy(r):
        return remote(agbuf.at[g], agbuf.at[g], s_a.at[r], r_a.at[r], group_peer(r))

    start_all(GROUP, a_copy)
    wait_recv(GROUP, a_copy)
    gp_out[...] = agbuf[...].astype(F32).reshape(FEAT, COLS)

    for h in range(2):
        for a in range(3):
            wait_recv(HEADS, out_copy(a, h))
            out_own(a, h).wait()
            wait_send(HEADS, out_copy(a, h))
            wait_send(HEADS, qkv_copy(a, h))
    wait_send(GROUP, a_copy)
    wait_send(GROUP, g_copy)
    wait_send(DP, x_copy)
    wait_send(DP, p_copy)
    wait_send(GROUP, rew_copy)
    for c in (c_up, c_dn, c_sib, f_up, f_dn, sib_dn, sib_up, sib_op):
        c.wait_send()


def local(queries, keys, values, noise, projection, rewards, counts, step_index):
    base = jnp.full((8, 128), step_factor(step_index, GROUP), F32)
    rew = jnp.full((8, 128), rewards[0, 0], F32)
    slot = jnp.arange(TXT, dtype=jnp.int32)
    bias = jnp.broadcast_to(jnp.where(slot < counts[0], 0.0, masked_score).astype(F32)[:, None], (TXT, CH))
    grad = jax.ShapeDtypeStruct((1, 1, TOK, HW), BF)
    hbm = pl.BlockSpec(memory_space=pl.ANY)
    vmem = pl.BlockSpec(memory_space=pltpu.VMEM)
    dma = pltpu.SemaphoreType.DMA
    return pl.pallas_call(
        kernel,
        out_shape=(grad, grad, grad, jax.ShapeDtypeStruct((FEAT, COLS), F32)),
        in_specs=[hbm] * 5 + [vmem] * 3,
        out_specs=(hbm, hbm, hbm, vmem),
        scratch_shapes=[
            pltpu.VMEM((3, 2, SEQ, HD), BF),
            pltpu.VMEM((SEQ, D), BF),
            pltpu.VMEM((FEAT, D), BF),
            pltpu.VMEM((GROUP, 8, 128), F32),
            pltpu.VMEM((2, NCH, SEQ, CH), F32),
            pltpu.VMEM((2, HD, SEQ), BF),
            pltpu.VMEM((2, HD, SEQ), BF),
            pltpu.VMEM((NCH, FEAT, CH), BF),
            pltpu.VMEM((NCH, FEAT, CH), BF),
            pltpu.VMEM((DP, FEAT, COLS), F32),
            pltpu.VMEM((DP, FEAT, COLS), BF),
            pltpu.VMEM((DP, FEAT, COLS), BF),
            pltpu.VMEM((GROUP, 16, COLS), BF),
            pltpu.VMEM((GROUP, 16, COLS), BF),
            pltpu.VMEM((GROUP, 16, COLS), BF),
            pltpu.VMEM((3, 2, SEQ, HD), BF),
            pltpu.VMEM((SEQ, HD), F32),
            pltpu.VMEM((SEQ, HD), F32),
            dma((3, 2, HEADS)), dma((3, 2, HEADS)),
            dma((3,)), dma((3,)),
            dma((2,)), dma((2,)),
            dma((4,)), dma((4,)),
            dma((DP,)), dma((DP,)),
            dma((GROUP,)), dma((GROUP,)),
            dma((DP,)), dma((DP,)),
            dma((GROUP,)), dma((GROUP,)),
            dma((GROUP,)), dma((GROUP,)),
            dma((3, 2, HEADS)), dma((3, 2, HEADS)),
        ],
        compiler_params=pltpu.CompilerParams(
            collective_id=0, has_side_effects=True, vmem_limit_bytes=58 << 20
        ),
        name="rollout_grads",
    )(queries, keys, values, noise, projection, rew, base, bias)


def solution(mesh):
    in_specs = (
        P("dp", "group", "head", None),
        P("dp", "group", "head", None),
        P("dp", "group", "head", None),
        P("dp", "group", "head", None),
        P("head", "dp"),
        P("dp", "group"),
        P("dp"),
        P(),
    )
    out_specs = (
        P("dp", "group", "head", None),
        P("dp", "group", "head", None),
        P("dp", "group", "head", None),
        P("head", "dp"),
    )
    return jax.shard_map(local, mesh=mesh, in_specs=in_specs, out_specs=out_specs, check_vma=False)
```

time: 455 us -> 177 us (0.39)
  the two profiles are of different devices: /device:TPU:2 before, /device:TPU:1 now
where the time goes in v1:
time: 177 us; the launch traced here: 175 us
  Pallas kernels  166 us (94%)
  local copies, waits for them, and re-layouts  6.37 us (4%)
  between operations  2.74 us (2%)
    pallas_call x1, Pallas kernels, local(): pl.pallas_call(kernel, out_shape=(grad, grad, grad, jax.ShapeDtypeStruct(...  166 us
    unnamed x10, local copies, waits for them, and re-layouts  4.44 us

profile of v1, /device:TPU:1, one launch (start us, length us, event | category | flops | bytes accessed | tf_op | source)
XLA Modules:
  0.0 175.4 jit_solution(12209780918318230396)
XLA Ops:
  2.7 0.6 broadcast_in_dim.20.rew_in
  3.3 0.6 broadcast_in_dim.21.base_in
  3.9 0.7 broadcast_in_dim.24.bias_in
  4.6 166.3 %rollout_grads.1 = (bf16[1,1,128,2048]{3,2,1,0:T(8,128)(2,1)}, bf16[1,1,128,2048]{3,2,1,0:T(8,128)(2,1)}, bf16[1,1,128,2048]{3,2,1,0:T(8,128)(2,1)}, f32[256,768]{1,0:T(8,128)}) custom-call(bf16[1,1,128,2048]{3,2,1,0:T(8,128)(2,1)} %q_in.1, bf16[1,1,128,2048]{3,2,1,0:T(8,128)(2,1)} %k_in.1, bf16[1,1,128,2048]{3,2,1,0:T(8,128)(2,1)} %v_in.1, ...), custom_call_target="tpu_custom_call" | custom-call | tf_op jit(solution)/shard_map/rollout_grads/pallas_call | solution.py:366
  171.0 0.0 copy-start.2
  171.0 0.0 copy-start.1
  171.0 2.0 %copy.19 = bf16[1,1,128,2048]{3,2,1,0:T(8,128)(2,1)} copy(bf16[1,1,128,2048]{3,2,1,0:T(8,128)(2,1)} %get-tuple-element.8) | data formatting | bytes 1048576
  172.9 0.0 copy-done.2
  173.0 0.0 copy-start
  173.0 0.8 copy.20
  173.7 0.0 copy-done.1
  173.8 0.8 copy.21
  174.5 0.0 copy-done
  174.5 0.9 copy.22
  (1 shorter events, 0.0 us)
Async XLA Ops:
  171.0 2.0 %copy-start.2 = (bf16[1,1,128,2048]{3,2,1,0:T(8,128)(2,1)S(1)}, bf16[1,1,128,2048]{3,2,1,0:T(8,128)(2,1)}, u32[]{:S(2)}) copy-start(bf16[1,1,128,2048]{3,2,1,0:T(8,128)(2,1)} %get-tuple-element.9) | copy-start | bytes 1572868
  171.0 2.8 %copy-start.1 = (bf16[1,1,128,2048]{3,2,1,0:T(8,128)(2,1)S(1)}, bf16[1,1,128,2048]{3,2,1,0:T(8,128)(2,1)}, u32[]{:S(2)}) copy-start(bf16[1,1,128,2048]{3,2,1,0:T(8,128)(2,1)} %get-tuple-element.10) | copy-start | bytes 1572868
  173.0 1.6 copy-start

commit v2 on v1

v2 whole, which is shorter than its diff:
```python
import functools
import math

import jax
import jax.numpy as jnp
from jax import lax
from jax.experimental import pallas as pl
from jax.experimental.pallas import tpu as pltpu
from jax.sharding import PartitionSpec as P

HD = 128
TXT = 128
NSTEPS = 50
SEQ = 1024
HW = 2048
D = 3072
HEADS = 8
DP = 4
GROUP = 16
TOK = SEQ // HEADS
FEAT = HW // HEADS
COLS = D // DP
CH = 256
NCH = SEQ // CH

shift_factor = 7.0
noise_level = 0.7
loss_scale = 64.0
spread_floor = 0.25
masked_score = -1e30

BF = jnp.bfloat16
F32 = jnp.float32
MESH = pl.DeviceIdType.MESH


def step_factor(step_index, rollout_count):
    current = step_index[0].astype(F32)

    def level_at(position):
        remain = 1.0 - position / NSTEPS
        return shift_factor * remain / (1.0 + (shift_factor - 1.0) * remain)

    stride = level_at(current) - level_at(current + 1.0)
    return loss_scale * jnp.sqrt(stride) / (noise_level * rollout_count)


def dot(a, b, ca, cb):
    return lax.dot_general(a, b, (((ca,), (cb,)), ((), ())), preferred_element_type=F32)


def kernel(
    q_in, k_in, v_in, n_in, p_in, rew_in, base_in, bias_in,
    gq_out, gk_out, gv_out, gp_out,
    qkv, nx, pcol, rbuf, fbuf, probs, kt, vt, out_t, part_s, part_own, part_r, dout_s, dout_t, oz, ox, wlow, yrecv, zlow, zrecv, agbuf,
    grads, acc_k, acc_v,
    s_qkv, r_qkv, s_nx, r_nx, s_ns, r_ns, s_p1, r_p1, s_up, r_up, s_dn, r_dn, s_pt, r_pt,
    s_rew, r_rew, s_f, r_f, s_d, r_d, s_out, r_out, s_x, r_x, s_y, r_y, s_z, r_z, s_a, r_a, s_o, r_o,
):
    x = lax.axis_index("dp")
    g = lax.axis_index("group")
    me = lax.axis_index("head")
    y = g // 2
    zlo = lax.rem(g, 2)
    zhi = me // 2
    core = lax.rem(me, 2)
    sib = me + 1 - 2 * core

    def remote(src, dst, ssem, rsem, dev):
        return pltpu.make_async_remote_copy(
            src_ref=src, dst_ref=dst, send_sem=ssem, recv_sem=rsem, device_id=dev, device_id_type=MESH
        )

    def head_peer(r):
        return (x, g, lax.rem(me + r, HEADS))

    def zhi_peer(r):
        return (x, g, lax.rem(me + 2 * r, HEADS))

    def dp_peer(r):
        return (lax.rem(x + r, DP), g, me)

    def group_peer(r):
        return (x, lax.rem(g + r, GROUP), me)

    def y_peer(r):
        return (x, lax.rem(g + 2 * r, GROUP), me)

    def z_place(r):
        return lax.rem(2 * zhi + zlo + r, 8)

    def z_peer(r):
        place = z_place(r)
        return (x, 2 * y + lax.rem(place, 2), 2 * (place // 2) + core)

    def rows(block, size):
        return pl.ds(pl.multiple_of(block * size, size), size)

    def each(count, make, *acts):
        def body(r, carry):
            copy = make(r)
            for act in acts:
                getattr(copy, act)()
            return carry

        lax.fori_loop(1, count, body, 0)

    barrier = pltpu.get_barrier_semaphore()

    def greet(count, peer):
        def body(r, carry):
            pl.semaphore_signal(barrier, inc=1, device_id=peer(r), device_id_type=MESH)
            return carry

        lax.fori_loop(1, count, body, 0)

    greet(HEADS, head_peer)
    greet(DP, dp_peer)
    greet(GROUP, group_peer)

    def far_peer(r):
        return (x, g + 1 - 2 * zlo, lax.rem(me + 2 * r, HEADS))

    greet(4, far_peer)
    pl.semaphore_wait(barrier, HEADS + DP + GROUP + 4 - 4)

    xcols = pl.ds(pl.multiple_of(x * COLS, COLS), COLS)

    def p1_copy(r):
        return remote(p_in.at[y], pcol.at[y, zhi], s_p1.at[r], r_p1.at[r], zhi_peer(r))

    each(4, p1_copy, "start")
    p_own = pltpu.make_async_copy(p_in, pcol.at[:, zhi], s_p1.at[0])
    p_own.start()

    def nx_copy(r):
        dst = lax.rem(x + r, DP)
        cols = pl.ds(pl.multiple_of(dst * COLS, COLS), COLS)
        return remote(
            n_in.at[0, 0, :, cols], nx.at[x, rows(core, TOK)], s_nx.at[r], r_nx.at[r], (dst, g, me)
        )

    each(DP, nx_copy, "start")
    nx_own = pltpu.make_async_copy(n_in.at[0, 0, :, xcols], nx.at[x, rows(core, TOK)], s_nx.at[0])
    nx_own.start()

    def rew_copy(r):
        return remote(rew_in, rbuf.at[r], s_rew.at[r], r_rew.at[r], group_peer(r))

    each(GROUP, rew_copy, "start")

    ins = (q_in, k_in, v_in)

    def qkv_copy(a, h):
        def make(r):
            dst = lax.rem(me + r, HEADS)
            cols = pl.ds(pl.multiple_of(dst * FEAT + h * HD, HD), HD)
            return remote(
                ins[a].at[0, 0, :, cols], qkv.at[a, h, rows(me, TOK)],
                s_qkv.at[a, h, r], r_qkv.at[a, h, r], (x, g, dst),
            )

        return make

    def qkv_own(a, h):
        cols = pl.ds(pl.multiple_of(me * FEAT + h * HD, HD), HD)
        return pltpu.make_async_copy(
            ins[a].at[0, 0, :, cols], qkv.at[a, h, rows(me, TOK)], s_qkv.at[a, h, 0]
        )

    def start_head(h):
        for a in range(3):
            each(HEADS, qkv_copy(a, h), "start")
            qkv_own(a, h).start()

    def ring_up(d, j):
        part = pcol.at[lax.rem(y + 8 - d, 8), lax.rem(zhi + 1 + j, 4)]
        return remote(part, part, s_up.at[d, j], r_up.at[d, j], y_peer(1))

    def ring_dn(d, j):
        part = pcol.at[lax.rem(y + d, 8), lax.rem(zhi + 1 + j, 4)]
        return remote(part, part, s_dn.at[d, j], r_dn.at[d, j], y_peer(7))

    def up_hop(d, j):
        return d < 3 or (d == 3 and j < 2)

    def dn_hop(d, j):
        return d < 3 or (d == 3 and j == 2)

    each(4, p1_copy, "wait_recv")
    for j in range(3):
        ring_up(0, j).start()
        ring_dn(0, j).start()
    start_head(0)

    each(GROUP, rew_copy, "wait_recv")
    rbuf[0] = rew_in[...]
    rewards = rbuf[...]
    average = jnp.sum(rewards, axis=0) / GROUP
    variance = jnp.sum((rewards - average[None]) ** 2, axis=0) / GROUP
    fbuf[x] = base_in[...] * ((rew_in[...] - average) / jnp.maximum(jnp.sqrt(variance), spread_floor))

    def f_copy(r):
        return remote(fbuf.at[x], fbuf.at[x], s_f.at[r], r_f.at[r], dp_peer(r))

    each(DP, f_copy, "start")
    factor = fbuf[x][0:1, :]

    each(DP, nx_copy, "wait_recv")
    nx_own.wait()
    nx_part = nx.at[:, rows(core, TOK)]
    nx_sib = remote(nx_part, nx_part, s_ns.at[0], r_ns.at[0], (x, g, sib))
    nx_sib.start()

    p_own.wait()

    def part_copy(b):
        def make(r):
            dst = lax.rem(x + r, DP)
            return remote(
                part_s.at[dst, :, rows(b, 32)], part_r.at[r, :, rows(b, 32)],
                s_pt.at[b, r], r_pt.at[b, r], (dst, g, me),
            )

        return make

    def make_part(blocks):
        lhs = jnp.concatenate([pcol[b].reshape(4 * 32, COLS) for b in blocks], axis=0)

        def body(r, carry):
            k = lax.rem(x + r, DP)
            part = dot(lhs, nx[k], 1, 1)
            low = part.astype(BF)
            for i, b in enumerate(blocks):
                for z in range(4):
                    part_s[k, z, rows(b, 32), :] = low[i * 128 + z * 32 : i * 128 + (z + 1) * 32]
            return carry

        lax.fori_loop(1, DP, body, 0)
        part = dot(lhs, nx[x], 1, 1)
        for i, b in enumerate(blocks):
            for z in range(4):
                part_own[z, rows(b, 32), :] = part[i * 128 + z * 32 : i * 128 + (z + 1) * 32]
        for b in blocks:
            each(DP, part_copy(b), "start")

    def sum_parts():
        def body(b, carry):
            each(DP, part_copy(b), "wait_recv")
            return carry

        lax.fori_loop(0, 8, body, 0)
        for z in range(4):
            total = part_own[z]
            for r in range(1, DP):
                total = total + part_r[r, z].astype(F32)
            dout_s[z] = total.astype(BF)

    scale = HD ** (-0.5)

    def out_copy(h):
        def make(r):
            dst = lax.rem(zhi + r, 4)
            return remote(
                out_t.at[dst, pl.ds(h * HD, HD)], oz.at[zhi, pl.ds(h * HD, HD)],
                s_out.at[h, r], r_out.at[h, r], zhi_peer(r),
            )

        return make

    def out_own(h):
        return pltpu.make_async_copy(
            out_t.at[zhi, pl.ds(h * HD, HD)], oz.at[zhi, pl.ds(h * HD, HD)], s_out.at[h, 0]
        )

    def forward_head(h):
        for a in range(3):
            qkv_own(a, h).wait()
            each(HEADS, qkv_copy(a, h), "wait_recv")
        kt[h] = qkv[1, h].T
        vt[h] = qkv[2, h].T

        def body(c, carry):
            qc = qkv[0, h, rows(c, CH), :]
            t = dot(qkv[1, h], qc, 1, 1) * (scale * math.log2(math.e))
            t = jnp.concatenate([t[: SEQ - TXT], t[SEQ - TXT :] + bias_in[...]], axis=0)
            peak = jnp.max(t, axis=0, keepdims=True)
            e = jnp.exp2(t - peak)
            total = jnp.sum(e, axis=0, keepdims=True)
            pr = e * (1.0 / total)
            probs[h, c] = pr
            part = dot(vt[h], pr.astype(BF), 1, 0)
            out_t[c, pl.ds(h * HD, HD), :] = part.astype(BF)
            return carry

        lax.fori_loop(0, NCH, body, 0)
        each(4, out_copy(h), "start")
        out_own(h).start()

    def ring_step(d):
        for j in range(3):
            if up_hop(d - 1, j):
                ring_up(d - 1, j).wait_recv()
                if up_hop(d, j):
                    ring_up(d, j).start()
            if dn_hop(d - 1, j):
                ring_dn(d - 1, j).wait_recv()
                if dn_hop(d, j):
                    ring_dn(d, j).start()

    def x_copy(h):
        part = oz.at[:, pl.ds(h * HD, HD)]

        def make(r):
            return remote(part, ox.at[x, :, pl.ds(h * HD, HD)], s_x.at[h, r], r_x.at[h, r], dp_peer(r))

        return make

    def x_own(h):
        return pltpu.make_async_copy(
            oz.at[:, pl.ds(h * HD, HD)], ox.at[x, :, pl.ds(h * HD, HD)], s_x.at[h, 0]
        )

    def share_out(h):
        out_own(h).wait()
        each(4, out_copy(h), "wait_recv")
        each(DP, x_copy(h), "start")
        x_own(h).start()

    def y_copy(h):
        def make(r):
            dst = lax.rem(y + r, 8)
            return remote(
                wlow.at[h, :, rows(dst, 16)], yrecv.at[h, r], s_y.at[h, r], r_y.at[h, r], y_peer(r)
            )

        return make

    def weight(h):
        x_own(h).wait()
        each(DP, x_copy(h), "wait_recv")

        def body(z, carry):
            total = jnp.zeros((HD, COLS), F32)
            for k in range(DP):
                part = dot(ox[k, z, pl.ds(h * HD, HD), :], nx[k], 1, 0)
                total = total + part * fbuf[k][0:1, 0:1]
            wlow[h, z] = total.astype(BF)
            return carry

        lax.fori_loop(0, 4, body, 0)
        each(8, y_copy(h), "start")

    nx_sib.wait_recv()
    make_part([y])
    ring_step(1)
    make_part([lax.rem(y + 7, 8), lax.rem(y + 1, 8)])
    ring_step(2)
    make_part([lax.rem(y + 6, 8), lax.rem(y + 2, 8)])
    ring_step(3)
    make_part([lax.rem(y + 5, 8), lax.rem(y + 3, 8)])
    ring_step(4)
    make_part([lax.rem(y + 4, 8)])

    def d_copy(r):
        dst = lax.rem(zhi + r, 4)
        return remote(dout_s.at[dst], dout_t.at[zhi], s_d.at[r], r_d.at[r], zhi_peer(r))

    start_head(1)
    forward_head(0)
    sum_parts()
    each(4, d_copy, "start")
    d_own = pltpu.make_async_copy(dout_s.at[zhi], dout_t.at[zhi], s_d.at[0])
    d_own.start()
    share_out(0)
    forward_head(1)
    each(DP, f_copy, "wait_recv")
    weight(0)
    share_out(1)

    outs = (gq_out, gk_out, gv_out)

    def grad_copy(a, h):
        cols = pl.ds(pl.multiple_of(me * FEAT + h * HD, HD), HD)

        def make(r):
            dst = lax.rem(me + r, HEADS)
            return remote(
                grads.at[a, h, rows(dst, TOK)], outs[a].at[0, 0, :, cols],
                s_o.at[a, h, r], r_o.at[a, h, r], (x, g, dst),
            )

        return make

    def grad_own(a, h):
        cols = pl.ds(pl.multiple_of(me * FEAT + h * HD, HD), HD)
        return pltpu.make_async_copy(
            grads.at[a, h, rows(me, TOK)], outs[a].at[0, 0, :, cols], s_o.at[a, h, 0]
        )

    def backward_head(h):
        acc_k[...] = jnp.zeros_like(acc_k)
        acc_v[...] = jnp.zeros_like(acc_v)

        def body(c, carry):
            pr = probs[h, c]
            dt = dout_t[c, pl.ds(h * HD, HD), :]
            ot = out_t[c, pl.ds(h * HD, HD), :]
            row_dot = jnp.sum(dt.astype(F32) * ot.astype(F32), axis=0, keepdims=True)
            dp = dot(qkv[2, h], dt, 1, 0)
            ds = (pr * (dp - row_dot)).astype(BF)
            gqt = dot(kt[h], ds, 1, 0)
            grads[0, h, rows(c, CH), :] = (gqt.T * (scale * factor)).astype(BF)
            acc_k[...] += dot(ds, qkv[0, h, rows(c, CH), :], 1, 0)
            acc_v[...] += dot(pr.astype(BF), dt, 1, 1)
            return carry

        lax.fori_loop(0, NCH, body, 0)
        grads[1, h] = (acc_k[...] * (scale * factor)).astype(BF)
        grads[2, h] = (acc_v[...] * factor).astype(BF)
        for a in range(3):
            each(HEADS, grad_copy(a, h), "start")
            grad_own(a, h).start()

    d_own.wait()
    each(4, d_copy, "wait_recv")
    backward_head(0)
    backward_head(1)
    weight(1)

    for h in range(2):
        each(8, y_copy(h), "wait_recv")
        total = wlow[h, :, rows(y, 16), :].astype(F32)
        for r in range(1, 8):
            total = total + yrecv[h, r].astype(F32)
        for z in range(4):
            zlow[2 * z + h] = total[z].astype(BF)

    def z_copy(r):
        return remote(zlow.at[z_place(r)], zrecv.at[r], s_z.at[r], r_z.at[r], z_peer(r))

    each(8, z_copy, "start")
    each(8, z_copy, "wait_recv")
    part = zlow[2 * zhi + zlo].astype(F32)
    for r in range(1, 8):
        part = part + zrecv[r].astype(F32)
    place = zlo * 8 + y
    agbuf[place] = part.astype(BF)

    def a_copy(r):
        return remote(agbuf.at[place], agbuf.at[place], s_a.at[r], r_a.at[r], group_peer(r))

    each(GROUP, a_copy, "start")
    each(GROUP, a_copy, "wait_recv")
    gp_out[...] = agbuf[...].astype(F32).reshape(FEAT, COLS)

    for h in range(2):
        for a in range(3):
            grad_own(a, h).wait()
            each(HEADS, grad_copy(a, h), "wait_recv", "wait_send")
            each(HEADS, qkv_copy(a, h), "wait_send")
        each(4, out_copy(h), "wait_send")
        each(DP, x_copy(h), "wait_send")
        each(8, y_copy(h), "wait_send")
    for j in range(3):
        for d in range(4):
            if up_hop(d, j):
                ring_up(d, j).wait_send()
            if dn_hop(d, j):
                ring_dn(d, j).wait_send()
    each(4, p1_copy, "wait_send")
    each(DP, nx_copy, "wait_send")
    each(DP, f_copy, "wait_send")
    each(GROUP, rew_copy, "wait_send")
    each(4, d_copy, "wait_send")
    each(8, z_copy, "wait_send")
    each(GROUP, a_copy, "wait_send")
    for b in range(8):
        each(DP, part_copy(b), "wait_send")
    nx_sib.wait_send()


def local(queries, keys, values, noise, projection, rewards, counts, step_index):
    base = jnp.full((8, 128), step_factor(step_index, GROUP), F32)
    rew = jnp.full((8, 128), rewards[0, 0], F32)
    slot = jnp.arange(TXT, dtype=jnp.int32)
    bias = jnp.broadcast_to(jnp.where(slot < counts[0], 0.0, masked_score).astype(F32)[:, None], (TXT, CH))
    grad = jax.ShapeDtypeStruct((1, 1, TOK, HW), BF)
    hbm = pl.BlockSpec(memory_space=pl.ANY)
    vmem = pl.BlockSpec(memory_space=pltpu.VMEM)
    dma = pltpu.SemaphoreType.DMA
    return pl.pallas_call(
        kernel,
        out_shape=(grad, grad, grad, jax.ShapeDtypeStruct((FEAT, COLS), F32)),
        in_specs=[hbm] * 5 + [vmem] * 3,
        out_specs=(hbm, hbm, hbm, vmem),
        scratch_shapes=[
            pltpu.VMEM((3, 2, SEQ, HD), BF),
            pltpu.VMEM((DP, 2 * TOK, COLS), BF),
            pltpu.VMEM((8, 4, 32, COLS), BF),
            pltpu.VMEM((GROUP, 8, 128), F32),
            pltpu.VMEM((DP, 8, 128), F32),
            pltpu.VMEM((2, NCH, SEQ, CH), F32),
            pltpu.VMEM((2, HD, SEQ), BF),
            pltpu.VMEM((2, HD, SEQ), BF),
            pltpu.VMEM((NCH, FEAT, CH), BF),
            pltpu.VMEM((DP, NCH, FEAT, CH), BF),
            pltpu.VMEM((NCH, FEAT, CH), F32),
            pltpu.VMEM((DP, NCH, FEAT, CH), BF),
            pltpu.VMEM((NCH, FEAT, CH), BF),
            pltpu.VMEM((NCH, FEAT, CH), BF),
            pltpu.VMEM((NCH, FEAT, CH), BF),
            pltpu.VMEM((DP, NCH, FEAT, CH), BF),
            pltpu.VMEM((2, 4, HD, COLS), BF),
            pltpu.VMEM((2, 8, 4, 16, COLS), BF),
            pltpu.VMEM((8, 16, COLS), BF),
            pltpu.VMEM((8, 16, COLS), BF),
            pltpu.VMEM((GROUP, 16, COLS), BF),
            pltpu.VMEM((3, 2, SEQ, HD), BF),
            pltpu.VMEM((SEQ, HD), F32),
            pltpu.VMEM((SEQ, HD), F32),
            dma((3, 2, HEADS)), dma((3, 2, HEADS)),
            dma((DP,)), dma((DP,)),
            dma((1,)), dma((1,)),
            dma((4,)), dma((4,)),
            dma((4, 3)), dma((4, 3)),
            dma((4, 3)), dma((4, 3)),
            dma((8, DP)), dma((8, DP)),
            dma((GROUP,)), dma((GROUP,)),
            dma((DP,)), dma((DP,)),
            dma((4,)), dma((4,)),
            dma((2, 4)), dma((2, 4)),
            dma((2, DP)), dma((2, DP)),
            dma((2, 8)), dma((2, 8)),
            dma((8,)), dma((8,)),
            dma((GROUP,)), dma((GROUP,)),
            dma((3, 2, HEADS)), dma((3, 2, HEADS)),
        ],
        compiler_params=pltpu.CompilerParams(
            collective_id=0, has_side_effects=True, vmem_limit_bytes=58 << 20
        ),
        name="rollout_grads",
    )(queries, keys, values, noise, projection.reshape(8, 32, COLS), rew, base, bias)


def solution(mesh):
    in_specs = (
        P("dp", "group", "head", None),
        P("dp", "group", "head", None),
        P("dp", "group", "head", None),
        P("dp", "group", "head", None),
        P("head", "dp"),
        P("dp", "group"),
        P("dp"),
        P(),
    )
    out_specs = (
        P("dp", "group", "head", None),
        P("dp", "group", "head", None),
        P("dp", "group", "head", None),
        P("head", "dp"),
    )
    return jax.shard_map(local, mesh=mesh, in_specs=in_specs, out_specs=out_specs, check_vma=False)
```

time: 177 us -> 160 us (0.904)
  Pallas kernels: 166 us -> 150 us
    pallas_call x1, Pallas kernels: 166 us -> 150 us  [local(): pl.pallas_call(kernel, out_shape=(grad, grad, grad, jax.ShapeDtypeStruct(...]
where the time goes in v2:
time: 160 us; the launch traced here: 159 us
  Pallas kernels  150 us (94%)
  local copies, waits for them, and re-layouts  6.37 us (4%)
  between operations  2.74 us (2%)
    pallas_call x1, Pallas kernels, local(): pl.pallas_call(kernel, out_shape=(grad, grad, grad, jax.ShapeDtypeStruct(...  150 us
    unnamed x10, local copies, waits for them, and re-layouts  4.44 us

profile of v2, /device:TPU:1, one launch (start us, length us, event | category | flops | bytes accessed | tf_op | source)
XLA Modules:
  0.0 159.4 jit_solution(695947065935063355)
XLA Ops:
  2.7 0.6 broadcast_in_dim.20.rew_in
  3.3 0.6 broadcast_in_dim.21.base_in
  3.9 0.7 broadcast_in_dim.24.bias_in
  4.6 150.3 %rollout_grads.1 = (bf16[1,1,128,2048]{3,2,1,0:T(8,128)(2,1)}, bf16[1,1,128,2048]{3,2,1,0:T(8,128)(2,1)}, bf16[1,1,128,2048]{3,2,1,0:T(8,128)(2,1)}, f32[256,768]{1,0:T(8,128)}) custom-call(bf16[1,1,128,2048]{3,2,1,0:T(8,128)(2,1)} %q_in.1, bf16[1,1,128,2048]{3,2,1,0:T(8,128)(2,1)} %k_in.1, bf16[1,1,128,2048]{3,2,1,0:T(8,128)(2,1)} %v_in.1, ...), custom_call_target="tpu_custom_call" | custom-call | tf_op jit(solution)/shard_map/rollout_grads/pallas_call | solution.py:492
  154.9 0.0 copy-start.2
  154.9 0.0 copy-start.1
  154.9 2.0 %copy.19 = bf16[1,1,128,2048]{3,2,1,0:T(8,128)(2,1)} copy(bf16[1,1,128,2048]{3,2,1,0:T(8,128)(2,1)} %get-tuple-element.8) | data formatting | bytes 1048576
  156.9 0.0 copy-done.2
  156.9 0.0 copy-start
  156.9 0.8 copy.20
  157.7 0.0 copy-done.1
  157.7 0.8 copy.21
  158.5 0.0 copy-done
  158.5 0.9 copy.22
  (1 shorter events, 0.0 us)
Async XLA Ops:
  154.9 2.0 %copy-start.2 = (bf16[1,1,128,2048]{3,2,1,0:T(8,128)(2,1)S(1)}, bf16[1,1,128,2048]{3,2,1,0:T(8,128)(2,1)}, u32[]{:S(2)}) copy-start(bf16[1,1,128,2048]{3,2,1,0:T(8,128)(2,1)} %get-tuple-element.9) | copy-start | bytes 1572868
  154.9 2.8 %copy-start.1 = (bf16[1,1,128,2048]{3,2,1,0:T(8,128)(2,1)S(1)}, bf16[1,1,128,2048]{3,2,1,0:T(8,128)(2,1)}, u32[]{:S(2)}) copy-start(bf16[1,1,128,2048]{3,2,1,0:T(8,128)(2,1)} %get-tuple-element.10) | copy-start | bytes 1572868
  156.9 1.6 %copy-start = (f32[256,768]{1,0:T(8,128)S(1)}, f32[256,768]{1,0:T(8,128)}, u32[]{:S(2)}) copy-start(f32[256,768]{1,0:T(8,128)} %get-tuple-element.11) | copy-start | bytes 2359300

commit v3 on v2

v3 whole, which is shorter than its diff:
```python
import functools
import math

import jax
import jax.numpy as jnp
from jax import lax
from jax.experimental import pallas as pl
from jax.experimental.pallas import tpu as pltpu
from jax.sharding import PartitionSpec as P

HD = 128
TXT = 128
NSTEPS = 50
SEQ = 1024
HW = 2048
D = 3072
HEADS = 8
DP = 4
GROUP = 16
TOK = SEQ // HEADS
FEAT = HW // HEADS
COLS = D // DP
CH = 256
NCH = SEQ // CH

shift_factor = 7.0
noise_level = 0.7
loss_scale = 64.0
spread_floor = 0.25
masked_score = -1e30

BF = jnp.bfloat16
F32 = jnp.float32
MESH = pl.DeviceIdType.MESH


def step_factor(step_index, rollout_count):
    current = jnp.full((8, 128), step_index.astype(F32), F32)

    def level_at(position):
        remain = 1.0 - position / NSTEPS
        return shift_factor * remain / (1.0 + (shift_factor - 1.0) * remain)

    stride = level_at(current) - level_at(current + 1.0)
    return loss_scale * jnp.sqrt(stride) / (noise_level * rollout_count)


def dot(a, b, ca, cb):
    return lax.dot_general(a, b, (((ca,), (cb,)), ((), ())), preferred_element_type=F32)


def kernel(
    q_in, k_in, v_in, n_in, p_in, rew_sm, count_sm, step_sm,
    g_out, gp_out,
    stage, qkv, nx, p_own, pring, bias_in, rbuf, fbuf, probs, kt, vt, out_t, part_s, part_own, part_r, dout_s, dout_t,
    oz, ox, wlow, yrecv, zlow, zrecv, agbuf, grads, acc_k, acc_v,
    s_in, s_qkv, r_qkv, s_nx, r_nx, s_ns, r_ns, s_p1, r_p1, s_up, r_up, s_dn, r_dn, s_pt, r_pt,
    s_rew, r_rew, s_f, r_f, s_d, r_d, s_out, r_out, s_x, r_x, s_y, r_y, s_z, r_z, s_a, r_a, s_o, r_o,
):
    x = lax.axis_index("dp")
    g = lax.axis_index("group")
    me = lax.axis_index("head")
    y = g // 2
    zlo = lax.rem(g, 2)
    zhi = me // 2
    core = lax.rem(me, 2)
    sib = me + 1 - 2 * core

    def remote(src, dst, ssem, rsem, dev):
        return pltpu.make_async_remote_copy(
            src_ref=src, dst_ref=dst, send_sem=ssem, recv_sem=rsem, device_id=dev, device_id_type=MESH
        )

    def head_peer(r):
        return (x, g, lax.rem(me + r, HEADS))

    def zhi_peer(r):
        return (x, g, lax.rem(me + 2 * r, HEADS))

    def dp_peer(r):
        return (lax.rem(x + r, DP), g, me)

    def y_peer(r):
        return (x, lax.rem(g + 2 * r, GROUP), me)

    def group_peer(r):
        return (x, lax.rem(g + r, GROUP), me)

    def z_peer(r):
        place = lax.rem(2 * zhi + zlo + r, 8)
        return (x, 2 * y + lax.rem(place, 2), 2 * (place // 2) + core)

    zlo_peer = (x, g + 1 - 2 * zlo, me)

    def rows(block, size):
        return pl.ds(pl.multiple_of(block * size, size), size)

    def each(count, make, *acts):
        def body(r, carry):
            copy = make(r)
            for act in acts:
                getattr(copy, act)()
            return carry

        lax.fori_loop(1, count, body, 0)

    barrier = pltpu.get_barrier_semaphore()

    def greet(count, peer):
        def body(r, carry):
            pl.semaphore_signal(barrier, inc=1, device_id=peer(r), device_id_type=MESH)
            return carry

        lax.fori_loop(1, count, body, 0)

    greet(HEADS, head_peer)
    greet(DP, dp_peer)
    greet(GROUP, group_peer)
    greet(4, lambda r: (x, g + 1 - 2 * zlo, lax.rem(me + 2 * r, HEADS)))

    xcols = pl.ds(pl.multiple_of(x * COLS, COLS), COLS)
    stages = [
        pltpu.make_async_copy(ref.at[0, 0], stage.at[a], s_in.at[a]) for a, ref in enumerate((q_in, k_in, v_in))
    ]
    nx_own = pltpu.make_async_copy(n_in.at[0, 0, :, xcols], nx.at[x, rows(core, TOK)], s_in.at[3])
    p_copy = pltpu.make_async_copy(p_in, p_own, s_in.at[4])
    for copy in stages:
        copy.start()
    nx_own.start()
    p_copy.start()
    rbuf[zlo, y] = jnp.full((8, 128), rew_sm[0, 0], F32)
    slot_row = lax.broadcasted_iota(jnp.int32, (TXT, CH), 0)
    bias_in[...] = jnp.where(slot_row < count_sm[0], 0.0, masked_score).astype(F32)
    pl.semaphore_wait(barrier, 7 + 3 + 15 + 3)

    def p1_copy(r):
        return remote(p_in.at[y], pring.at[y, 3 - r], s_p1.at[r], r_p1.at[r], zhi_peer(r))

    each(4, p1_copy, "start")

    def nx_copy(r):
        dst = lax.rem(x + r, DP)
        cols = pl.ds(pl.multiple_of(dst * COLS, COLS), COLS)
        return remote(
            n_in.at[0, 0, :, cols], nx.at[x, rows(core, TOK)], s_nx.at[r], r_nx.at[r], (dst, g, me)
        )

    each(DP, nx_copy, "start")
    rew_part = rbuf.at[zlo, y]
    rew_first = remote(rew_part, rew_part, s_rew.at[0], r_rew.at[0], zlo_peer)
    rew_first.start()

    pieces = ((0, 3, 0), (0, 2, 1), (2, 1, 1))

    def qkv_copy(i):
        first, count, h = pieces[i]

        def make(r):
            dst = lax.rem(me + r, HEADS)
            cols = pl.ds(pl.multiple_of(dst * FEAT + h * HD, HD), HD)
            return remote(
                stage.at[pl.ds(first, count), :, cols], qkv.at[pl.ds(first, count), h, rows(me, TOK)],
                s_qkv.at[i, r], r_qkv.at[i, r], (x, g, dst),
            )

        return make

    def qkv_own(h):
        cols = pl.ds(pl.multiple_of(me * FEAT + h * HD, HD), HD)
        return pltpu.make_async_copy(stage.at[:, :, cols], qkv.at[:, h, rows(me, TOK)], s_qkv.at[h, 0])

    def ring_up(d):
        part = pring.at[lax.rem(y + 8 - d, 8)]
        if d == 3:
            part = part.at[pl.ds(0, 2)]
        return remote(part, part, s_up.at[d], r_up.at[d], y_peer(1))

    def ring_dn(d):
        part = pring.at[lax.rem(y + d, 8)]
        if d == 3:
            part = part.at[pl.ds(2, 1)]
        return remote(part, part, s_dn.at[d], r_dn.at[d], y_peer(7))

    for copy in stages:
        copy.wait()
    each(HEADS, qkv_copy(0), "start")
    each(HEADS, qkv_copy(1), "start")
    for h in range(2):
        qkv_own(h).start()
    each(4, p1_copy, "wait_recv")
    ring_up(0).start()
    ring_dn(0).start()

    nx_own.wait()
    p_copy.wait()
    each(DP, nx_copy, "wait_recv")
    nx_part = nx.at[:, rows(core, TOK)]
    nx_sib = remote(nx_part, nx_part, s_ns.at[0], r_ns.at[0], (x, g, sib))
    nx_sib.start()
    rew_first.wait_recv()

    def rew_copy(r):
        part = rbuf.at[:, y]
        return remote(part, part, s_rew.at[r], r_rew.at[r], y_peer(r))

    each(8, rew_copy, "start")

    def part_copy(first, count, sem):
        def make(r):
            dst = lax.rem(x + r, DP)
            return remote(
                part_s.at[dst, pl.ds(first, count)], part_r.at[r, pl.ds(first, count)],
                s_pt.at[sem, r], r_pt.at[sem, r], (dst, g, me),
            )

        return make

    order = [y] + [lax.rem(y + k, 8) for k in (7, 1, 6, 2, 5, 3, 4)]
    part_groups = ((0, 1), (1, 2), (3, 2), (5, 3))

    def make_part(first, count):
        blocks = [v for b in order[first : first + count] for v in (p_own[b], pring[b].reshape(3 * 32, COLS))]
        lhs = jnp.concatenate(blocks, axis=0)

        def body(r, carry):
            k = lax.rem(x + r, DP)
            part_s[k, pl.ds(first, count)] = dot(lhs, nx[k], 1, 1).astype(BF).reshape(count, HD, CH)
            return carry

        lax.fori_loop(1, DP, body, 0)
        part_own[pl.ds(first, count)] = dot(lhs, nx[x], 1, 1).reshape(count, HD, CH)

    def sum_parts():
        for i, group in enumerate(part_groups):
            each(DP, part_copy(*group, i), "wait_recv")
            for k in range(group[0], group[0] + group[1]):
                total = part_own[k]
                for r in range(1, DP):
                    total = total + part_r[r, k].astype(F32)
                low = total.astype(BF)
                for z in range(4):
                    dout_s[z, rows(order[k], 32), :] = low[z * 32 : (z + 1) * 32]

    scale = HD ** (-0.5)

    def out_copy(h):
        def make(r):
            dst = lax.rem(zhi + r, 4)
            return remote(
                out_t.at[dst, pl.ds(h * HD, HD)], oz.at[zhi, pl.ds(h * HD, HD)],
                s_out.at[h, r], r_out.at[h, r], zhi_peer(r),
            )

        return make

    def out_own(h):
        return pltpu.make_async_copy(
            out_t.at[zhi, pl.ds(h * HD, HD)], oz.at[zhi, pl.ds(h * HD, HD)], s_out.at[h, 0]
        )

    def forward_head(h):
        qkv_own(h).wait()
        for i in ((0,), (1, 2))[h]:
            each(HEADS, qkv_copy(i), "wait_recv")
        kt[h] = qkv[1, h].T
        vt[h] = qkv[2, h].T

        def body(c, carry):
            qc = qkv[0, h, rows(c, CH), :]
            t = dot(qkv[1, h], qc, 1, 1) * (scale * math.log2(math.e))
            t = jnp.concatenate([t[: SEQ - TXT], t[SEQ - TXT :] + bias_in[...]], axis=0)
            peak = jnp.max(t, axis=0, keepdims=True)
            e = jnp.exp2(t - peak)
            total = jnp.sum(e, axis=0, keepdims=True)
            pr = e * (1.0 / total)
            probs[h, c] = pr
            part = dot(vt[h], pr.astype(BF), 1, 0)
            out_t[c, pl.ds(h * HD, HD), :] = part.astype(BF)
            return carry

        lax.fori_loop(0, NCH, body, 0)
        each(4, out_copy(h), "start")
        out_own(h).start()

    def ring_step(d):
        ring_up(d - 1).wait_recv()
        if d < 4:
            ring_up(d).start()
        ring_dn(d - 1).wait_recv()
        if d < 4:
            ring_dn(d).start()

    halves = ((0, 4), (0, 2), (2, 2))

    def x_copy(i):
        first, count = halves[i]
        feats = pl.ds(min(i, 1) * HD, HD)

        def make(r):
            return remote(
                oz.at[pl.ds(first, count), feats], ox.at[x, pl.ds(first, count), feats],
                s_x.at[i, r], r_x.at[i, r], dp_peer(r),
            )

        return make

    def x_own(h):
        feats = pl.ds(h * HD, HD)
        return pltpu.make_async_copy(oz.at[:, feats], ox.at[x, :, feats], s_x.at[h, 0])

    def share_out(h):
        out_own(h).wait()
        each(4, out_copy(h), "wait_recv")
        x_own(h).start()
        for i in ((0,), (1, 2))[h]:
            each(DP, x_copy(i), "start")

    def y_copy(i):
        first, count = halves[i]
        h = min(i, 1)

        def make(r):
            dst = lax.rem(y + r, 8)
            return remote(
                wlow.at[h, pl.ds(first, count), rows(dst, 16)], yrecv.at[h, r, pl.ds(first, count)],
                s_y.at[i, r], r_y.at[i, r], y_peer(r),
            )

        return make

    def weight(i):
        first, count = halves[i]
        h = min(i, 1)
        if i < 2:
            x_own(h).wait()
        each(DP, x_copy(i), "wait_recv")

        def body(z, carry):
            total = jnp.zeros((HD, COLS), F32)
            for k in range(DP):
                part = dot(ox[k, z, pl.ds(h * HD, HD), :], nx[k], 1, 0)
                total = total + part * fbuf[k][0:1, 0:1]
            wlow[h, z] = total.astype(BF)
            return carry

        lax.fori_loop(first, first + count, body, 0)
        each(8, y_copy(i), "start")

    def d_copy(h):
        feats = pl.ds(h * HD, HD)

        def make(r):
            return remote(
                dout_s.at[r, feats], dout_t.at[zhi, feats], s_d.at[h, r], r_d.at[h, r], zhi_peer(r)
            )

        return make

    def d_own(h):
        feats = pl.ds(h * HD, HD)
        return pltpu.make_async_copy(dout_s.at[0, feats], dout_t.at[zhi, feats], s_d.at[h, 0])

    def f_copy(r):
        return remote(fbuf.at[x], fbuf.at[x], s_f.at[r], r_f.at[r], dp_peer(r))

    def make_factor():
        each(8, rew_copy, "wait_recv")
        rewards = rbuf[...].reshape(GROUP, 8, 128)
        average = jnp.sum(rewards, axis=0) / GROUP
        variance = jnp.sum((rewards - average[None]) ** 2, axis=0) / GROUP
        base = step_factor(step_sm[0], GROUP)
        fbuf[x] = base * ((rbuf[zlo, y] - average) / jnp.maximum(jnp.sqrt(variance), spread_floor))
        each(DP, f_copy, "start")

    grad_pieces = ((0, 3, 0), (0, 1, 1), (1, 1, 1), (2, 1, 1))

    def grad_copy(i):
        first, count, h = grad_pieces[i]
        cols = pl.ds(pl.multiple_of(me * FEAT + h * HD, HD), HD)

        def make(r):
            dst = lax.rem(me + r, HEADS)
            return remote(
                grads.at[pl.ds(first, count), h, rows(dst, TOK)], g_out.at[pl.ds(first, count), :, cols],
                s_o.at[i, r], r_o.at[i, r], (x, g, dst),
            )

        return make

    def grad_own(h):
        cols = pl.ds(pl.multiple_of(me * FEAT + h * HD, HD), HD)
        return pltpu.make_async_copy(grads.at[:, h, rows(me, TOK)], g_out.at[:, :, cols], s_o.at[h, 0])

    def backward_head(h):
        factor = fbuf[x][0:1, :]
        acc_k[...] = jnp.zeros_like(acc_k)
        acc_v[...] = jnp.zeros_like(acc_v)

        def body(c, carry):
            pr = probs[h, c]
            dt = dout_t[c, pl.ds(h * HD, HD), :]
            ot = out_t[c, pl.ds(h * HD, HD), :]
            row_dot = jnp.sum(dt.astype(F32) * ot.astype(F32), axis=0, keepdims=True)
            dp = dot(qkv[2, h], dt, 1, 0)
            ds = (pr * (dp - row_dot)).astype(BF)
            gqt = dot(kt[h], ds, 1, 0)
            grads[0, h, rows(c, CH), :] = (gqt.T * (scale * factor)).astype(BF)
            acc_k[...] += dot(ds, qkv[0, h, rows(c, CH), :], 1, 0)
            acc_v[...] += dot(pr.astype(BF), dt, 1, 1)
            return carry

        lax.fori_loop(0, NCH, body, 0)
        grads[1, h] = (acc_k[...] * (scale * factor)).astype(BF)
        grads[2, h] = (acc_v[...] * factor).astype(BF)
        grad_own(h).start()

    def add_y(h):
        for i in ((0,), (1, 2))[h]:
            each(8, y_copy(i), "wait_recv")
        total = wlow[h, :, rows(y, 16), :].astype(F32)
        for r in range(1, 8):
            total = total + yrecv[h, r].astype(F32)
        for z in range(4):
            zlow[2 * z + h] = total[z].astype(BF)

    def z_copy(r):
        return remote(
            zlow.at[lax.rem(2 * zhi + zlo + r, 8)], zrecv.at[r], s_z.at[r], r_z.at[r], z_peer(r)
        )

    nx_sib.wait_recv()
    make_part(*part_groups[0])
    each(DP, part_copy(*part_groups[0], 0), "start")
    ring_step(1)
    make_part(*part_groups[1])
    each(DP, part_copy(*part_groups[1], 1), "start")
    ring_step(2)
    make_part(*part_groups[2])
    each(DP, part_copy(*part_groups[2], 2), "start")
    ring_step(3)
    forward_head(0)
    each(HEADS, qkv_copy(2), "start")
    ring_step(4)
    make_part(*part_groups[3])
    each(DP, part_copy(*part_groups[3], 3), "start")
    make_factor()
    sum_parts()
    each(4, d_copy(0), "start")
    d_own(0).start()
    share_out(0)
    forward_head(1)
    each(4, d_copy(1), "start")
    d_own(1).start()
    each(DP, f_copy, "wait_recv")
    weight(0)
    share_out(1)
    d_own(0).wait()
    each(4, d_copy(0), "wait_recv")
    backward_head(0)
    each(HEADS, grad_copy(0), "start")
    weight(1)
    weight(2)
    d_own(1).wait()
    each(4, d_copy(1), "wait_recv")
    backward_head(1)
    each(HEADS, grad_copy(1), "start")
    add_y(0)
    add_y(1)
    each(8, z_copy, "start")
    each(HEADS, grad_copy(2), "start")
    each(HEADS, grad_copy(3), "start")

    for h in range(2):
        each(4, out_copy(h), "wait_send")
        each(4, d_copy(h), "wait_send")
    for i in range(3):
        each(HEADS, qkv_copy(i), "wait_send")
        each(DP, x_copy(i), "wait_send")
        each(8, y_copy(i), "wait_send")
    for i, group in enumerate(part_groups):
        each(DP, part_copy(*group, i), "wait_send")
    for d in range(4):
        ring_up(d).wait_send()
        ring_dn(d).wait_send()
    each(4, p1_copy, "wait_send")
    each(DP, nx_copy, "wait_send")
    each(DP, f_copy, "wait_send")
    each(8, rew_copy, "wait_send")
    rew_first.wait_send()
    nx_sib.wait_send()

    each(8, z_copy, "wait_recv")
    part = zlow[2 * zhi + zlo].astype(F32)
    for r in range(1, 8):
        part = part + zrecv[r].astype(F32)
    agbuf[zlo, y] = part.astype(BF)

    def a_copy(r):
        part = agbuf.at[zlo, y]
        return remote(part, part, s_a.at[r], r_a.at[r], group_peer(r))

    each(GROUP, a_copy, "start")
    each(GROUP, a_copy, "wait_recv")
    gp_out[...] = agbuf[...].astype(F32).reshape(FEAT, COLS)

    for h in range(2):
        grad_own(h).wait()
    for i in range(4):
        each(HEADS, grad_copy(i), "wait_recv")
        each(HEADS, grad_copy(i), "wait_send")
    each(8, z_copy, "wait_send")
    each(GROUP, a_copy, "wait_send")


def local(queries, keys, values, noise, projection, rewards, counts, step_index):
    hbm = pl.BlockSpec(memory_space=pl.ANY)
    vmem = pl.BlockSpec(memory_space=pltpu.VMEM)
    smem = pl.BlockSpec(memory_space=pltpu.SMEM)
    dma = pltpu.SemaphoreType.DMA
    grads, grad_projection = pl.pallas_call(
        kernel,
        out_shape=(jax.ShapeDtypeStruct((3, TOK, HW), BF), jax.ShapeDtypeStruct((FEAT, COLS), F32)),
        in_specs=[hbm] * 5 + [smem] * 3,
        out_specs=(hbm, vmem),
        scratch_shapes=[
            pltpu.VMEM((3, TOK, HW), BF),
            pltpu.VMEM((3, 2, SEQ, HD), BF),
            pltpu.VMEM((DP, 2 * TOK, COLS), BF),
            pltpu.VMEM((8, 32, COLS), BF),
            pltpu.VMEM((8, 3, 32, COLS), BF),
            pltpu.VMEM((TXT, CH), F32),
            pltpu.VMEM((2, 8, 8, 128), F32),
            pltpu.VMEM((DP, 8, 128), F32),
            pltpu.VMEM((2, NCH, SEQ, CH), F32),
            pltpu.VMEM((2, HD, SEQ), BF),
            pltpu.VMEM((2, HD, SEQ), BF),
            pltpu.VMEM((NCH, FEAT, CH), BF),
            pltpu.VMEM((DP, 8, HD, CH), BF),
            pltpu.VMEM((8, HD, CH), F32),
            pltpu.VMEM((DP, 8, HD, CH), BF),
            pltpu.VMEM((NCH, FEAT, CH), BF),
            pltpu.VMEM((NCH, FEAT, CH), BF),
            pltpu.VMEM((NCH, FEAT, CH), BF),
            pltpu.VMEM((DP, NCH, FEAT, CH), BF),
            pltpu.VMEM((2, 4, HD, COLS), BF),
            pltpu.VMEM((2, 8, 4, 16, COLS), BF),
            pltpu.VMEM((8, 16, COLS), BF),
            pltpu.VMEM((8, 16, COLS), BF),
            pltpu.VMEM((2, 8, 16, COLS), BF),
            pltpu.VMEM((3, 2, SEQ, HD), BF),
            pltpu.VMEM((SEQ, HD), F32),
            pltpu.VMEM((SEQ, HD), F32),
            dma((5,)),
            dma((3, HEADS)), dma((3, HEADS)),
            dma((DP,)), dma((DP,)),
            dma((1,)), dma((1,)),
            dma((4,)), dma((4,)),
            dma((4,)), dma((4,)),
            dma((4,)), dma((4,)),
            dma((4, DP)), dma((4, DP)),
            dma((8,)), dma((8,)),
            dma((DP,)), dma((DP,)),
            dma((2, 4)), dma((2, 4)),
            dma((2, 4)), dma((2, 4)),
            dma((3, DP)), dma((3, DP)),
            dma((3, 8)), dma((3, 8)),
            dma((8,)), dma((8,)),
            dma((GROUP,)), dma((GROUP,)),
            dma((4, HEADS)), dma((4, HEADS)),
        ],
        compiler_params=pltpu.CompilerParams(
            collective_id=0, has_side_effects=True, vmem_limit_bytes=58 << 20
        ),
        name="rollout_grads",
    )(queries, keys, values, noise, projection.reshape(8, 32, COLS), rewards, counts, step_index)
    return (*(grads[a][None, None] for a in range(3)), grad_projection)


def solution(mesh):
    in_specs = (
        P("dp", "group", "head", None),
        P("dp", "group", "head", None),
        P("dp", "group", "head", None),
        P("dp", "group", "head", None),
        P("head", "dp"),
        P("dp", "group"),
        P("dp"),
        P(),
    )
    out_specs = (
        P("dp", "group", "head", None),
        P("dp", "group", "head", None),
        P("dp", "group", "head", None),
        P("head", "dp"),
    )
    return jax.shard_map(local, mesh=mesh, in_specs=in_specs, out_specs=out_specs, check_vma=False)
```

time: 160 us -> 147 us (0.919)
  Pallas kernels: 150 us -> 140 us
  local copies, waits for them, and re-layouts: 6.37 us -> 3.5 us
    pallas_call x1, Pallas kernels: 150 us -> 140 us  [local(): pl.pallas_call(kernel, out_shape=(jax.ShapeDtypeStruct((3, TOK, HW), BF),...]
    unnamed x10 -> x3, local copies, waits for them, and re-layouts: 4.44 us -> 0.88 us
    another operation x0 -> x1, local copies, waits for them, and re-layouts: none -> 2.62 us  [local(): return (*(grads[a][None, None] for a in range(3)), grad_projection)]
    broadcast_in_dim x3 -> x0, local copies, waits for them, and re-layouts: 1.93 us -> none  [the longest x1 0.74 us: local(): jnp.broadcast_to(jnp.where(slot < counts[0], 0.0, masked_score).astype(F3...]
where the time goes in v3:
time: 147 us; the launch traced here: 146 us
  Pallas kernels  140 us (95%)
  local copies, waits for them, and re-layouts  3.5 us (2%)
  between operations  2.59 us (2%)
    pallas_call x1, Pallas kernels, local(): pl.pallas_call(kernel, out_shape=(jax.ShapeDtypeStruct((3, TOK, HW), BF),...  140 us

profile of v3, /device:TPU:1, one launch (start us, length us, event | category | flops | bytes accessed | tf_op | source)
XLA Modules:
  0.0 146.5 jit_solution(1291289953339839989)
XLA Ops:
  2.6 140.4 %rollout_grads.1 = (bf16[3,128,2048]{2,1,0:T(8,128)(2,1)}, f32[256,768]{1,0:T(8,128)}) custom-call(bf16[1,1,128,2048]{3,2,1,0:T(8,128)(2,1)} %q_in.1, bf16[1,1,128,2048]{3,2,1,0:T(8,128)(2,1)} %k_in.1, bf16[1,1,128,2048]{3,2,1,0:T(8,128)(2,1)} %v_in.1, bf16[1,1,128,3072]{3,2,1,0:T(8,128)(2,1)} %n_in.1, bf16[8,32,768]{2,1,0:T(8,128)(2,1)} %bitcast.7, ...), custom_call_target="tpu_custom_call" | custom-call | tf_op jit(solution)/shard_map/rollout_grads/pallas_call | solution.py:520
  143.0 0.0 copy-start
  143.0 2.6 %slice_bitcast_fusion = (bf16[1,1,128,2048]{3,2,1,0:T(8,128)(2,1)}, bf16[1,1,128,2048]{3,2,1,0:T(8,128)(2,1)}, bf16[1,1,128,2048]{3,2,1,0:T(8,128)(2,1)}) fusion(bf16[3,128,2048]{2,1,0:T(8,128)(2,1)} %get-tuple-element.6), kind=kLoop, calls=%fused_computation | loop fusion | bytes 3145728 | tf_op jit(solution)/shard_map/broadcast_in_dim;squeeze | solution.py:576
  145.6 0.0 copy-done
  145.6 0.9 copy.16
Async XLA Ops:
  143.0 2.6 %copy-start = (f32[256,768]{1,0:T(8,128)S(1)}, f32[256,768]{1,0:T(8,128)}, u32[]{:S(2)}) copy-start(f32[256,768]{1,0:T(8,128)} %get-tuple-element.18) | copy-start | bytes 2359300

commit v4 on v3

--- a/solution.py
+++ b/solution.py
@@ -150,7 +150,7 @@
     rew_first = remote(rew_part, rew_part, s_rew.at[0], r_rew.at[0], zlo_peer)
     rew_first.start()
 
-    pieces = ((0, 3, 0), (0, 2, 1), (2, 1, 1))
+    pieces = ((0, 3, 0), (0, 1, 1), (1, 2, 1))
 
     def qkv_copy(i):
         first, count, h = pieces[i]
@@ -427,6 +427,31 @@
         return remote(
             zlow.at[lax.rem(2 * zhi + zlo + r, 8)], zrecv.at[r], s_z.at[r], r_z.at[r], z_peer(r)
         )
+
+    def send_z(h):
+        @pl.when(zlo == h)
+        def near():
+            for r in (2, 4, 6):
+                z_copy(r).start()
+
+        @pl.when(zlo != h)
+        def far():
+            for r in (1, 3, 5, 7):
+                z_copy(r).start()
+
+    def a_copy(r):
+        part = agbuf.at[zlo, y]
+        return remote(part, part, s_a.at[r], r_a.at[r], group_peer(r))
+
+    def add_z(h):
+        @pl.when(zlo == h)
+        def last():
+            each(8, z_copy, "wait_recv")
+            part = zlow[2 * zhi + zlo].astype(F32)
+            for r in range(1, 8):
+                part = part + zrecv[r].astype(F32)
+            agbuf[zlo, y] = part.astype(BF)
+            each(GROUP, a_copy, "start")
 
     nx_sib.wait_recv()
     make_part(*part_groups[0])
@@ -444,11 +469,11 @@
     make_part(*part_groups[3])
     each(DP, part_copy(*part_groups[3], 3), "start")
     make_factor()
+    share_out(0)
     sum_parts()
+    forward_head(1)
     each(4, d_copy(0), "start")
     d_own(0).start()
-    share_out(0)
-    forward_head(1)
     each(4, d_copy(1), "start")
     d_own(1).start()
     each(DP, f_copy, "wait_recv")
@@ -460,14 +485,17 @@
     each(HEADS, grad_copy(0), "start")
     weight(1)
     weight(2)
+    add_y(0)
+    send_z(0)
     d_own(1).wait()
     each(4, d_copy(1), "wait_recv")
     backward_head(1)
     each(HEADS, grad_copy(1), "start")
-    add_y(0)
+    add_z(0)
     add_y(1)
-    each(8, z_copy, "start")
+    send_z(1)
     each(HEADS, grad_copy(2), "start")
+    add_z(1)
     each(HEADS, grad_copy(3), "start")
 
     for h in range(2):
@@ -489,17 +517,6 @@
     rew_first.wait_send()
     nx_sib.wait_send()
 
-    each(8, z_copy, "wait_recv")
-    part = zlow[2 * zhi + zlo].astype(F32)
-    for r in range(1, 8):
-        part = part + zrecv[r].astype(F32)
-    agbuf[zlo, y] = part.astype(BF)
-
-    def a_copy(r):
-        part = agbuf.at[zlo, y]
-        return remote(part, part, s_a.at[r], r_a.at[r], group_peer(r))
-
-    each(GROUP, a_copy, "start")
     each(GROUP, a_copy, "wait_recv")
     gp_out[...] = agbuf[...].astype(F32).reshape(FEAT, COLS)
 

time: 147 us -> 143 us (0.973)
  Pallas kernels: 140 us -> 137 us
    pallas_call x1, Pallas kernels: 140 us -> 137 us  [local(): pl.pallas_call(kernel, out_shape=(jax.ShapeDtypeStruct((3, TOK, HW), BF),...]
where the time goes in v4:
time: 143 us
  Pallas kernels  137 us (96%)
  local copies, waits for them, and re-layouts  3.5 us (2%)
  between operations  2.59 us (2%)
    pallas_call x1, Pallas kernels, local(): pl.pallas_call(kernel, out_shape=(jax.ShapeDtypeStruct((3, TOK, HW), BF),...  137 us

profile of v4, /device:TPU:1, one launch (start us, length us, event | category | flops | bytes accessed | tf_op | source)
XLA Modules:
  0.0 142.9 jit_solution(3938266502660809307)
XLA Ops:
  2.6 136.9 %rollout_grads.1 = (bf16[3,128,2048]{2,1,0:T(8,128)(2,1)}, f32[256,768]{1,0:T(8,128)}) custom-call(bf16[1,1,128,2048]{3,2,1,0:T(8,128)(2,1)} %q_in.1, bf16[1,1,128,2048]{3,2,1,0:T(8,128)(2,1)} %k_in.1, bf16[1,1,128,2048]{3,2,1,0:T(8,128)(2,1)} %v_in.1, bf16[1,1,128,3072]{3,2,1,0:T(8,128)(2,1)} %n_in.1, bf16[8,32,768]{2,1,0:T(8,128)(2,1)} %bitcast.7, ...), custom_call_target="tpu_custom_call" | custom-call | tf_op jit(solution)/shard_map/rollout_grads/pallas_call | solution.py:537
  139.4 0.0 copy-start
  139.5 2.6 %slice_bitcast_fusion = (bf16[1,1,128,2048]{3,2,1,0:T(8,128)(2,1)}, bf16[1,1,128,2048]{3,2,1,0:T(8,128)(2,1)}, bf16[1,1,128,2048]{3,2,1,0:T(8,128)(2,1)}) fusion(bf16[3,128,2048]{2,1,0:T(8,128)(2,1)} %get-tuple-element.6), kind=kLoop, calls=%fused_computation | loop fusion | bytes 3145728 | tf_op jit(solution)/shard_map/broadcast_in_dim;squeeze | solution.py:593
  142.1 0.0 copy-done
  142.1 0.9 copy.16
Async XLA Ops:
  139.4 2.6 %copy-start = (f32[256,768]{1,0:T(8,128)S(1)}, f32[256,768]{1,0:T(8,128)}, u32[]{:S(2)}) copy-start(f32[256,768]{1,0:T(8,128)} %get-tuple-element.18) | copy-start | bytes 2359300

commit v5 on v4

--- a/solution.py
+++ b/solution.py
@@ -527,6 +527,17 @@
         each(HEADS, grad_copy(i), "wait_send")
     each(8, z_copy, "wait_send")
     each(GROUP, a_copy, "wait_send")
+
+
+def hand_out(grads, projection, gq_out, gk_out, gv_out, gp_out, sems):
+    copies = [
+        pltpu.make_async_copy(grads.at[a], out.at[0, 0], sems.at[a]) for a, out in enumerate((gq_out, gk_out, gv_out))
+    ]
+    copies.append(pltpu.make_async_copy(projection, gp_out, sems.at[3]))
+    for copy in copies:
+        copy.start()
+    for copy in copies:
+        copy.wait()
 
 
 def local(queries, keys, values, noise, projection, rewards, counts, step_index):
@@ -590,7 +601,15 @@
         ),
         name="rollout_grads",
     )(queries, keys, values, noise, projection.reshape(8, 32, COLS), rewards, counts, step_index)
-    return (*(grads[a][None, None] for a in range(3)), grad_projection)
+    grad = jax.ShapeDtypeStruct((1, 1, TOK, HW), BF)
+    return pl.pallas_call(
+        hand_out,
+        out_shape=(grad, grad, grad, jax.ShapeDtypeStruct((FEAT, COLS), F32)),
+        in_specs=[hbm] * 2,
+        out_specs=(hbm,) * 4,
+        scratch_shapes=[dma((4,))],
+        name="hand_out",
+    )(grads, grad_projection)
 
 
 def solution(mesh):

time: 143 us -> 212 us (1.48)
  Pallas kernels: 137 us -> 209 us
  local copies, waits for them, and re-layouts: 3.5 us -> 0 us
    pallas_call x0 -> x1, Pallas kernels: none -> 72.6 us  [local(): pl.pallas_call(hand_out, out_shape=(grad, grad, grad, jax.ShapeDtypeStruc...]
    another operation x1 -> x0, local copies, waits for them, and re-layouts: 2.62 us -> none  [local(): return (*(grads[a][None, None] for a in range(3)), grad_projection)]
where the time goes in v5:
time: 212 us
  Pallas kernels  209 us (99%)
  between operations  2.58 us (1%)
    pallas_call x1, Pallas kernels, local(): pl.pallas_call(kernel, out_shape=(jax.ShapeDtypeStruct((3, TOK, HW), BF),...  137 us
    pallas_call x1, Pallas kernels, local(): pl.pallas_call(hand_out, out_shape=(grad, grad, grad, jax.ShapeDtypeStruc...  72.6 us

profile of v5, /device:TPU:1, one launch (start us, length us, event | category | flops | bytes accessed | tf_op | source)
XLA Modules:
  0.0 212.1 jit_solution(6506297914040636678)
XLA Ops:
  2.6 136.9 %rollout_grads.1 = (bf16[3,128,2048]{2,1,0:T(8,128)(2,1)}, f32[256,768]{1,0:T(8,128)}) custom-call(bf16[1,1,128,2048]{3,2,1,0:T(8,128)(2,1)} %q_in.1, bf16[1,1,128,2048]{3,2,1,0:T(8,128)(2,1)} %k_in.1, bf16[1,1,128,2048]{3,2,1,0:T(8,128)(2,1)} %v_in.1, bf16[1,1,128,3072]{3,2,1,0:T(8,128)(2,1)} %n_in.1, bf16[8,32,768]{2,1,0:T(8,128)(2,1)} %bitcast.1, ...), custom_call_target="tpu_custom_call" | custom-call | tf_op jit(solution)/shard_map/rollout_grads/pallas_call | solution.py:548
  139.5 72.6 %hand_out.1 = (bf16[1,1,128,2048]{3,2,1,0:T(8,128)(2,1)}, bf16[1,1,128,2048]{3,2,1,0:T(8,128)(2,1)}, bf16[1,1,128,2048]{3,2,1,0:T(8,128)(2,1)}, f32[256,768]{1,0:T(8,128)}) custom-call(bf16[3,128,2048]{2,1,0:T(8,128)(2,1)} %get-tuple-element.6.grads, f32[256,768]{1,0:T(8,128)} %get-tuple-element.7.projection), custom_call_target="tpu_custom_call" | custom-call | tf_op jit(solution)/shard_map/hand_out/pallas_call | solution.py:605
